TPU v7x, 32 devices: a whole 2x2x4 slice. The times are simulated.
32 devices in a mesh: parts: 2 (over y), dp: 2 (over core), tensor: 8 (over z, x).
Axes of the slice: x: 2, y: 2, z: 4, core: 2. Of those that a mesh axis runs over, the one named last changes fastest.
Arguments:
- tokens: bfloat16 [4096, 6144], P(('parts', 'dp'), 'tensor'), parts along dimension 0, may hold values from -6 to 6
- expert_index: int32 [4096, 2], P(('parts', 'dp')), parts along dimension 0, may hold values from 0 to 7, as said below
- combine_weight: float32 [4096, 2], P(('parts', 'dp')), parts along dimension 0, may hold values from 0.2 to 1
- gate_weight: bfloat16 [6144, 16384], P(None, 'tensor'), may hold values from -0.078125 to 0.078125
- up_weight: bfloat16 [6144, 16384], P(None, 'tensor'), may hold values from -0.078125 to 0.078125
- down_weight: bfloat16 [16384, 6144], P('tensor'), may hold values from -0.0625 to 0.0625
Outputs:
- mixed: bfloat16 [4096, 6144], P(('parts', 'dp'), 'tensor'), parts along dimension 0
There are 2 independent parts, one for each index of `parts`. A program takes and returns all parts, laid end to end along the dimension named above; an argument that names none is the same for every part. Nothing has to cross between parts.
Inputs may be any that keep to these rules, and one draw needn't show every extreme that they name: `expert_index`: each row names 2 different experts. Among the tokens of one dp index (each aligned block of 1024 rows) at most 512 name expert 0, a quarter of 512 at least, and in every draw some block has exactly 512.
All inputs are finite; a program needn't handle non-finite values.
Results may differ from a plain program's by a relative error of at most 0.005.
Values may be sent and summed in bfloat16 or wider, within the bound.
No kernel may reach another device: no remote copies, remote signals or barrier semaphores. Data moves between devices by JAX's collectives and lax.ppermute only.
A program may use at most 192 MiB of HBM per device.

v0:
```python
import functools

import jax
import jax.numpy as jnp
from jax import lax
from jax.experimental import pallas as pl
from jax.experimental.pallas import tpu as pltpu
from jax.sharding import PartitionSpec as P

MOST = 512
LANES = 128
TILE = 256
WIDE = 512
COST = 2
F32 = jnp.float32
BF16 = jnp.bfloat16
VMEM_BYTES = 28 * 1024 * 1024


def params():
    return pltpu.CompilerParams(vmem_limit_bytes=VMEM_BYTES)


def dot(a, b):
    return jnp.dot(a, b, preferred_element_type=F32)


def compact_kernel(routed_ref, tokens_ref, chosen_ref, slot_ref, select_ref):
    slots = select_ref.shape[0]
    groups = routed_ref.shape[0]
    routed = routed_ref[...]
    above = lax.broadcasted_iota(jnp.int32, (LANES, LANES), 0) <= lax.broadcasted_iota(
        jnp.int32, (LANES, LANES), 1
    )
    within = dot(routed.astype(BF16), jnp.where(above, 1.0, 0.0).astype(BF16))
    before = jnp.zeros((1, 1), F32)
    slot_ids = lax.broadcasted_iota(jnp.int32, (slots, LANES), 0)
    for g in range(groups):
        row = within[g : g + 1, :] + before
        before = row[:, LANES - 1 :]
        slot = jnp.where(routed[g : g + 1, :] > 0, row.astype(jnp.int32) - 1, -1)
        slot_ref[g : g + 1, :] = slot
        select_ref[:, g * LANES : (g + 1) * LANES] = jnp.where(slot_ids == slot, 1.0, 0.0).astype(BF16)
    chosen_ref[...] = dot(select_ref[...], tokens_ref[...]).astype(BF16)


def compact(routed, tokens, slots):
    count, width = tokens.shape
    groups = count // LANES
    return pl.pallas_call(
        compact_kernel,
        out_shape=(
            jax.ShapeDtypeStruct((slots, width), BF16),
            jax.ShapeDtypeStruct((groups, LANES), jnp.int32),
        ),
        scratch_shapes=[pltpu.VMEM((slots, count), BF16)],
        compiler_params=params(),
        name="compact",
    )(routed.astype(F32).reshape(groups, LANES), tokens)


def silu(value):
    return value / (1.0 + jnp.exp(-value))


def gate_up_kernel(ids_ref, *refs, steps, pieces, first, last):
    xs, refs = refs[:pieces], refs[pieces:]
    gate_weight, up_weight, *refs = refs
    gate_in, up_in = (None, None) if first else refs[:2]
    refs = refs if first else refs[2:]
    hold, sem = refs[-2:]
    width = xs[0].shape[1]
    blocks, tile = hold.shape[0], hold.shape[-1]

    def copy(n, which, j):
        weight = (gate_weight, up_weight)[which]
        rows = pl.ds(pl.multiple_of(ids_ref[steps[j]] * width, width), width)
        columns = pl.ds(pl.multiple_of(n * tile, tile), tile)
        return pltpu.make_async_copy(
            weight.at[rows, columns],
            hold.at[n, which, j * width : (j + 1) * width],
            sem.at[n, which, j],
        )

    def begin(n, carry):
        for which in range(2):
            for j in range(len(steps)):
                copy(n, which, j).start()
        return carry

    def block(n, carry):
        at = pl.ds(pl.multiple_of(n * tile, tile), tile)
        x = jnp.concatenate([piece[...] for piece in xs], axis=0 if last else 1)
        values = []
        for which in range(2):
            for j in range(len(steps)):
                copy(n, which, j).wait()
            value = dot(x, hold[n, which])
            if not first:
                value = (gate_in, up_in)[which][:, at] + value
            values.append(value)
        if last:
            refs[0][:, at] = (silu(values[0]) * values[1]).astype(BF16)
        else:
            refs[0][:, at], refs[1][:, at] = values
        return carry

    lax.fori_loop(0, blocks, begin, 0)
    lax.fori_loop(0, blocks, block, 0)


def gate_up(ids, steps, xs, gate_weight, up_weight, sums, last=False):
    width = xs[0].shape[1]
    hidden = gate_weight.shape[1]
    slots = xs[0].shape[0] * (len(xs) if last else 1)
    first = sums is None
    on_chip = pl.BlockSpec(memory_space=pltpu.VMEM)
    away = pl.BlockSpec(memory_space=pl.ANY)
    operands = [*xs, gate_weight, up_weight, *([] if first else sums)]
    aliases = {}
    if last:
        out_shape, out_specs = jax.ShapeDtypeStruct((slots, hidden), BF16), on_chip
    else:
        out_shape = (pltpu.VMEM((slots, hidden), F32),) * 2
        out_specs = (on_chip, on_chip)
        if not first:
            at = 1 + len(operands) - 2
            aliases = {at: 0, at + 1: 1}
    blocks = hidden // WIDE
    flops = 4 * slots * width * hidden * len(steps)
    moved = 4 * width * hidden * len(steps)
    return pl.pallas_call(
        functools.partial(gate_up_kernel, steps=steps, pieces=len(xs), first=first, last=last),
        in_specs=[pl.BlockSpec(memory_space=pltpu.SMEM)]
        + [on_chip] * len(xs)
        + [away] * 2
        + [on_chip] * (0 if first else 2),
        out_specs=out_specs,
        out_shape=out_shape,
        scratch_shapes=[
            pltpu.VMEM((blocks, 2, width * len(steps), WIDE), BF16),
            pltpu.SemaphoreType.DMA((blocks, 2, len(steps))),
        ],
        input_output_aliases=aliases,
        compiler_params=params(),
        cost_estimate=pl.CostEstimate(flops=COST * flops, bytes_accessed=moved, transcendentals=0),
        name="gate_up",
    )(ids, *operands)


def down_kernel(ids_ref, hidden_ref, weight_ref, *refs, steps, split):
    outs, hold, sem = refs[:-2], *refs[-2:]
    width = hold.shape[-1]
    depth = hidden_ref.shape[1]
    cuts = sem.shape[1]
    deep = depth // cuts

    def copy(i, k):
        columns = pl.ds(pl.multiple_of(ids_ref[steps[i]] * width, width), width)
        rows = slice(k * deep, (k + 1) * deep)
        return pltpu.make_async_copy(weight_ref.at[rows, columns], hold.at[i, rows], sem.at[i, k])

    for i in range(len(steps)):
        for k in range(cuts):
            copy(i, k).start()
    for i in range(len(steps)):

        def block(n, carry, i=i):
            @pl.when(n == 0)
            def _():
                for k in range(cuts):
                    copy(i, k).wait()

            at = pl.ds(pl.multiple_of(n * TILE, TILE), TILE)
            value = dot(hidden_ref[...], hold[i, :, at])
            if split:
                rows = outs[0].shape[0]
                outs[0][:, at] = value[:rows].astype(BF16)
                outs[1][:, at] = value[rows:].astype(BF16)
            else:
                outs[i][:, at] = value
            return carry

        lax.fori_loop(0, width // TILE, block, 0)


def down(ids, steps, hidden, down_weight, width, split=False):
    slots, depth = hidden.shape
    if split:
        shape, kind, outs = (slots // 2, width), BF16, 2
    else:
        shape, kind, outs = (slots, width), F32, len(steps)
    on_chip = pl.BlockSpec(memory_space=pltpu.VMEM)
    return pl.pallas_call(
        functools.partial(down_kernel, steps=steps, split=split),
        in_specs=[pl.BlockSpec(memory_space=pltpu.SMEM), on_chip, pl.BlockSpec(memory_space=pl.ANY)],
        out_specs=(on_chip,) * outs,
        out_shape=(jax.ShapeDtypeStruct(shape, kind),) * outs,
        scratch_shapes=[
            pltpu.VMEM((len(steps), depth, width), BF16),
            pltpu.SemaphoreType.DMA((len(steps), 4)),
        ],
        compiler_params=params(),
        cost_estimate=pl.CostEstimate(
            flops=COST * 2 * slots * depth * width * len(steps),
            bytes_accessed=2 * depth * width * len(steps),
            transcendentals=0,
        ),
        name="down",
    )(ids, hidden, down_weight)


def spread_kernel(place_ref, scale_ref, own_ref, right_ref, left_ref, out_ref):
    total = own_ref[...] + right_ref[...].astype(F32) + left_ref[...].astype(F32)
    scaled = (total * scale_ref[...]).astype(BF16)
    out_ref[...] = dot(place_ref[...], scaled).astype(BF16)


def spread(place, scale, own, right, left):
    count, slots = place.shape
    width = own.shape[1]
    block = pl.BlockSpec((slots, TILE), lambda n: (0, n))
    return pl.pallas_call(
        spread_kernel,
        grid=(width // TILE,),
        in_specs=[
            pl.BlockSpec(place.shape, lambda n: (0, 0)),
            pl.BlockSpec(scale.shape, lambda n: (0, 0)),
            block,
            block,
            block,
        ],
        out_specs=pl.BlockSpec((count, TILE), lambda n: (0, n)),
        out_shape=jax.ShapeDtypeStruct((count, width), BF16),
        compiler_params=params(),
        name="spread",
    )(place, scale, own, right, left)


def ring_of(size):
    return [*range(0, size, 2), *range(size - 1, 0, -2)]


def ring_plan(size, slots, tokens, routed, factor, gate_weight, up_weight, down_weight):
    width = tokens.shape[1]
    half = size // 2
    order = ring_of(size)
    table = [[order[(order.index(me) + s) % size] for s in range(size)] for me in range(size)]
    ids = jnp.asarray(table, jnp.int32)[lax.axis_index("tensor")]
    to_right = [(order[i], order[(i + 1) % size]) for i in range(size)]
    to_left = [(b, a) for a, b in to_right]

    def right_of(value):
        return lax.ppermute(value, "tensor", to_right)

    def left_of(value):
        return lax.ppermute(value, "tensor", to_left)

    own, slot = compact(routed, tokens, slots)

    right, left = right_of(own), left_of(own)
    sums = gate_up(ids, [0], [own], gate_weight, up_weight, None)
    for s in range(1, half):
        here = [right, left]
        if s + 1 < half:
            right, left = right_of(right), left_of(left)
        else:
            right, left = right_of(right[: slots // 2]), left_of(left[slots // 2 :])
        sums = gate_up(ids, [size - s, s], here, gate_weight, up_weight, sums)
    hidden = gate_up(ids, [half], [right, left], gate_weight, up_weight, sums, last=True)

    top, bottom = down(ids, [half], hidden, down_weight, width, split=True)
    right, left = right_of(top), left_of(bottom)
    for s in range(half - 1, 0, -1):
        ahead, behind = down(ids, [s, size - s], hidden, down_weight, width)
        if s == half - 1:
            rows = slots // 2
            ahead = jnp.concatenate([ahead[:rows] + right.astype(F32), ahead[rows:]])
            behind = jnp.concatenate([behind[:rows], behind[rows:] + left.astype(F32)])
        else:
            ahead = ahead + right.astype(F32)
            behind = behind + left.astype(F32)
        right, left = right_of(ahead.astype(BF16)), left_of(behind.astype(BF16))
    (mine,) = down(ids, [0], hidden, down_weight, width)

    slot = slot.reshape(-1)
    slot_ids = jnp.arange(slots, dtype=jnp.int32)
    place = (slot[:, None] == slot_ids[None, :]).astype(BF16)
    scale = jnp.sum(jnp.where(slot_ids[:, None] == slot[None, :], factor[None, :], 0.0), axis=1)
    return spread(place, scale[:, None], mine, right, left)


def plain_plan(slots, tokens, routed, factor, gate_weight, up_weight, down_weight):
    slot = jnp.where(routed, jnp.cumsum(routed.astype(jnp.int32)) - 1, -1)
    slot_ids = jnp.arange(slots, dtype=jnp.int32)
    select = slot_ids[:, None] == slot[None, :]
    chosen = dot(select.astype(BF16), tokens).astype(BF16)
    scale = jnp.sum(jnp.where(select, factor[None, :], 0.0), axis=1)
    full = lax.all_gather(chosen, "tensor", axis=1, tiled=True)
    gate, up = dot(full, gate_weight), dot(full, up_weight)
    hidden = (jax.nn.silu(gate) * up).astype(BF16)
    partial = dot(hidden, down_weight) * scale[:, None]
    total = lax.psum_scatter(partial, "tensor", scatter_dimension=1, tiled=True)
    return dot(select.T.astype(BF16), total.astype(BF16)).astype(BF16)


def local(size, tokens, expert_index, combine_weight, gate_weight, up_weight, down_weight):
    chosen = expert_index == 0
    routed = jnp.any(chosen, axis=1)
    factor = jnp.sum(jnp.where(chosen, combine_weight, 0.0), axis=1)
    rest = (tokens, routed, factor, gate_weight, up_weight, down_weight)
    fits = (
        size >= 4
        and size % 2 == 0
        and tokens.shape[1] % TILE == 0
        and gate_weight.shape[1] % WIDE == 0
        and tokens.shape[0] % LANES == 0
    )
    if not fits:
        return plain_plan(MOST, *rest)
    return ring_plan(size, MOST, *rest)


def solution(mesh):
    rows = P(("parts", "dp"), "tensor")
    in_specs = (
        rows,
        P(("parts", "dp"), None),
        P(("parts", "dp"), None),
        P(None, "tensor"),
        P(None, "tensor"),
        P("tensor", None),
    )
    return jax.shard_map(
        functools.partial(local, mesh.shape["tensor"]),
        mesh=mesh,
        in_specs=in_specs,
        out_specs=rows,
        check_vma=False,
    )
```

profile of v0, /device:TPU:0, one launch (start us, length us, event | category | flops | bytes accessed | tf_op | source)
XLA Modules:
  0.0 155.8 jit_solution(13745857162112346830)
XLA Ops:
  0.0 0.7 fusion.1
  0.7 1.4 copy-done
  2.1 1.4 compact.1
  3.5 3.1 %collective-permute-start = (bf16[512,768]{1,0:T(8,128)(2,1)S(1)}, bf16[512,768]{1,0:T(8,128)(2,1)S(1)}, u32[]{:S(2)}, u32[]{:S(2)}) collective-permute-start(bf16[512,768]{1,0:T(8,128)(2,1)S(1)} %get-tuple-element.24.refs_0_), channel_id=1, source_target_pairs={{0,2},{2,4},{4,6},{6,7},{7,5},{5,3},{3,1},{1,0},{8,10},{10,12},{12... | collective-permute-start | bytes 2359304 | tf_op jit(solution)/shard_map/ppermute | solution.py:254
  6.6 0.7 dynamic-slice_bitcast_fusion.ids_ref
  7.3 6.5 %gate_up.5 = (f32[512,2048]{1,0:T(8,128)S(1)}, f32[512,2048]{1,0:T(8,128)S(1)}) custom-call(s32[8]{0:T(128)S(1)} %dynamic-slice_bitcast_fusion.ids_ref, bf16[512,768]{1,0:T(8,128)(2,1)S(1)} %get-tuple-element.24.refs_0_, bf16[6144,2048]{1,0:T(8,128)(2,1)} %refs_2_.9, bf16[6144,2048]{1,0:T(8,128)(2,1)} %refs_3_.7), custom_call_target="tpu_custom_call" | custom-call | flops 6442450944 | bytes 6291456 | tf_op jit(solution)/shard_map/gate_up/pallas_call | solution.py:132
  13.8 10.3 %collective-permute-done.refs_0_ = bf16[512,768]{1,0:T(8,128)(2,1)S(1)} collective-permute-done((bf16[512,768]{1,0:T(8,128)(2,1)S(1)}, bf16[512,768]{1,0:T(8,128)(2,1)S(1)}, u32[]{:S(2)}, u32[]{:S(2)}) %collective-permute-start) | collective-permute-done | bytes 786464 | tf_op jit(solution)/shard_map/ppermute | solution.py:254
  24.0 1.8 %collective-permute-start.1 = (bf16[512,768]{1,0:T(8,128)(2,1)S(1)}, bf16[512,768]{1,0:T(8,128)(2,1)S(1)}, u32[]{:S(2)}, u32[]{:S(2)}) collective-permute-start(bf16[512,768]{1,0:T(8,128)(2,1)S(1)} %collective-permute-done.refs_0_), channel_id=1, source_target_pairs={{0,2},{2,4},{4,6},{6,7},{7,5},{5,3},{3,1},{1,0},{8,10},{10,12},{12... | collective-permute-start | bytes 2359304 | tf_op jit(solution)/shard_map/ppermute | solution.py:254
  25.9 0.2 collective-permute-start.5
  26.1 10.7 %gate_up.6 = (f32[512,2048]{1,0:T(8,128)S(1)}, f32[512,2048]{1,0:T(8,128)S(1)}) custom-call(s32[8]{0:T(128)S(1)} %dynamic-slice_bitcast_fusion.ids_ref, bf16[512,768]{1,0:T(8,128)(2,1)S(1)} %collective-permute-done.refs_0_, bf16[512,768]{1,0:T(8,128)(2,1)S(1)} %collective-permute-done.4.refs_1_, ...), custom_call_target="tpu_custom_call", output_to_operand_aliasing={{0}: (5, {}), {1}: (6, {})} | custom-call | flops 12884901888 | bytes 12582912 | tf_op jit(solution)/shard_map/gate_up/pallas_call | solution.py:132
  36.8 6.0 %collective-permute-done.1.refs_0_ = bf16[512,768]{1,0:T(8,128)(2,1)S(1)} collective-permute-done((bf16[512,768]{1,0:T(8,128)(2,1)S(1)}, bf16[512,768]{1,0:T(8,128)(2,1)S(1)}, u32[]{:S(2)}, u32[]{:S(2)}) %collective-permute-start.1) | collective-permute-done | bytes 786464 | tf_op jit(solution)/shard_map/ppermute | solution.py:254
  42.8 1.5 collective-permute-start.2
  44.3 0.5 collective-permute-start.6
  44.8 10.7 %gate_up.7 = (f32[512,2048]{1,0:T(8,128)S(1)}, f32[512,2048]{1,0:T(8,128)S(1)}) custom-call(s32[8]{0:T(128)S(1)} %dynamic-slice_bitcast_fusion.ids_ref, bf16[512,768]{1,0:T(8,128)(2,1)S(1)} %collective-permute-done.1.refs_0_, bf16[512,768]{1,0:T(8,128)(2,1)S(1)} %collective-permute-done.5.refs_1_, ...), custom_call_target="tpu_custom_call", output_to_operand_aliasing={{0}: (5, {}), {1}: (6, {})} | custom-call | flops 12884901888 | bytes 12582912 | tf_op jit(solution)/shard_map/gate_up/pallas_call | solution.py:132
  55.5 5.1 %collective-permute-done.2.refs_0_ = bf16[512,768]{1,0:T(8,128)(2,1)S(1)} collective-permute-done((bf16[512,768]{1,0:T(8,128)(2,1)S(1)}, bf16[512,768]{1,0:T(8,128)(2,1)S(1)}, u32[]{:S(2)}, u32[]{:S(2)}) %collective-permute-start.2) | collective-permute-done | bytes 786464 | tf_op jit(solution)/shard_map/ppermute | solution.py:254
  60.6 1.4 collective-permute-start.3
  62.0 0.8 collective-permute-start.7
  62.8 10.7 %gate_up.8 = (f32[512,2048]{1,0:T(8,128)S(1)}, f32[512,2048]{1,0:T(8,128)S(1)}) custom-call(s32[8]{0:T(128)S(1)} %dynamic-slice_bitcast_fusion.ids_ref, bf16[512,768]{1,0:T(8,128)(2,1)S(1)} %collective-permute-done.2.refs_0_, bf16[512,768]{1,0:T(8,128)(2,1)S(1)} %collective-permute-done.6.refs_1_, ...), custom_call_target="tpu_custom_call", output_to_operand_aliasing={{0}: (5, {}), {1}: (6, {})} | custom-call | flops 12884901888 | bytes 12582912 | tf_op jit(solution)/shard_map/gate_up/pallas_call | solution.py:132
  73.5 7.0 %gate_up.9.hidden_ref = bf16[512,2048]{1,0:T(8,128)(2,1)S(1)} custom-call(s32[8]{0:T(128)S(1)} %dynamic-slice_bitcast_fusion.ids_ref, bf16[256,768]{1,0:T(8,128)(2,1)S(1)} %collective-permute-done.3.refs_0_, bf16[256,768]{1,0:T(8,128)(2,1)S(1)} %collective-permute-done.7.refs_1_, bf16[6144,2048]{1,0:T(8,128)(2,1)} %refs_2_.9, bf16[6144,2048]{1,0:T(8,128)(2,1)} %refs_3_.7, ...), custom_call_target="tpu_custom_call" | custom-call | flops 6442450944 | bytes 6291456 | tf_op jit(solution)/shard_map/gate_up/pallas_call | solution.py:132
  80.5 4.6 %down.9 = (bf16[256,768]{1,0:T(8,128)(2,1)S(1)}, bf16[256,768]{1,0:T(8,128)(2,1)S(1)}) custom-call(s32[8]{0:T(128)S(1)} %dynamic-slice_bitcast_fusion.ids_ref, bf16[512,2048]{1,0:T(8,128)(2,1)S(1)} %gate_up.9.hidden_ref, bf16[2048,6144]{1,0:T(8,128)(2,1)} %weight_ref.9), custom_call_target="tpu_custom_call" | custom-call | flops 3221225472 | bytes 3145728 | tf_op jit(solution)/shard_map/down/pallas_call | solution.py:194
  85.1 1.3 collective-permute-start.12
  86.4 6.8 %down.8 = (f32[512,768]{1,0:T(8,128)S(1)}, f32[512,768]{1,0:T(8,128)S(1)}) custom-call(s32[8]{0:T(128)S(1)} %dynamic-slice_bitcast_fusion.ids_ref, bf16[512,2048]{1,0:T(8,128)(2,1)S(1)} %gate_up.9.hidden_ref, bf16[2048,6144]{1,0:T(8,128)(2,1)} %weight_ref.9), custom_call_target="tpu_custom_call" | custom-call | flops 6442450944 | bytes 6291456 | tf_op jit(solution)/shard_map/down/pallas_call | solution.py:194
  93.3 0.8 collective-permute-start.8
  94.2 0.1 add_convert_fusion.4
  94.3 1.3 collective-permute-start.13
  95.6 7.7 %collective-permute-done.8 = bf16[256,768]{1,0:T(8,128)(2,1)S(1)} collective-permute-done((bf16[256,768]{1,0:T(8,128)(2,1)S(1)}, bf16[256,768]{1,0:T(8,128)(2,1)S(1)}, u32[]{:S(2)}, u32[]{:S(2)}) %collective-permute-start.8) | collective-permute-done | bytes 393248 | tf_op jit(solution)/shard_map/ppermute | solution.py:254
  103.3 0.1 add_convert_fusion.5
  103.4 0.4 collective-permute-start.9
  103.8 6.8 %down.7 = (f32[512,768]{1,0:T(8,128)S(1)}, f32[512,768]{1,0:T(8,128)S(1)}) custom-call(s32[8]{0:T(128)S(1)} %dynamic-slice_bitcast_fusion.ids_ref, bf16[512,2048]{1,0:T(8,128)(2,1)S(1)} %gate_up.9.hidden_ref, bf16[2048,6144]{1,0:T(8,128)(2,1)} %weight_ref.9), custom_call_target="tpu_custom_call" | custom-call | flops 6442450944 | bytes 6291456 | tf_op jit(solution)/shard_map/down/pallas_call | solution.py:194
  110.6 1.3 collective-permute-done.13
  111.8 0.2 add_convert_fusion.1
  112.0 1.3 collective-permute-start.14
  113.3 7.4 %collective-permute-done.9 = bf16[512,768]{1,0:T(8,128)(2,1)S(1)} collective-permute-done((bf16[512,768]{1,0:T(8,128)(2,1)S(1)}, bf16[512,768]{1,0:T(8,128)(2,1)S(1)}, u32[]{:S(2)}, u32[]{:S(2)}) %collective-permute-start.9) | collective-permute-done | bytes 786464 | tf_op jit(solution)/shard_map/ppermute | solution.py:254
  120.7 0.2 add_convert_fusion.3
  120.9 0.5 collective-permute-start.10
  121.5 6.8 %down.6 = (f32[512,768]{1,0:T(8,128)S(1)}, f32[512,768]{1,0:T(8,128)S(1)}) custom-call(s32[8]{0:T(128)S(1)} %dynamic-slice_bitcast_fusion.ids_ref, bf16[512,2048]{1,0:T(8,128)(2,1)S(1)} %gate_up.9.hidden_ref, bf16[2048,6144]{1,0:T(8,128)(2,1)} %weight_ref.9), custom_call_target="tpu_custom_call" | custom-call | flops 6442450944 | bytes 6291456 | tf_op jit(solution)/shard_map/down/pallas_call | solution.py:194
  128.3 0.2 collective-permute-done.14
  128.5 1.1 add_convert_fusion
  129.5 1.5 collective-permute-start.15
  131.1 6.5 %collective-permute-done.10 = bf16[512,768]{1,0:T(8,128)(2,1)S(1)} collective-permute-done((bf16[512,768]{1,0:T(8,128)(2,1)S(1)}, bf16[512,768]{1,0:T(8,128)(2,1)S(1)}, u32[]{:S(2)}, u32[]{:S(2)}) %collective-permute-start.10) | collective-permute-done | bytes 786464 | tf_op jit(solution)/shard_map/ppermute | solution.py:254
  137.6 1.0 add_convert_fusion.2
  138.7 0.3 collective-permute-start.11
  139.0 0.3 select_reduce_fusion
  139.3 0.1 copy.15.scale_ref
  139.4 0.2 fusion.place_ref
  139.7 4.6 %down.5.own_ref = f32[512,768]{1,0:T(8,128)S(1)} custom-call(s32[8]{0:T(128)S(1)} %dynamic-slice_bitcast_fusion.ids_ref, bf16[512,2048]{1,0:T(8,128)(2,1)S(1)} %gate_up.9.hidden_ref, bf16[2048,6144]{1,0:T(8,128)(2,1)} %weight_ref.9), custom_call_target="tpu_custom_call" | custom-call | flops 3221225472 | bytes 3145728 | tf_op jit(solution)/shard_map/down/pallas_call | solution.py:194
  144.3 7.5 %collective-permute-done.11.right_ref = bf16[512,768]{1,0:T(8,128)(2,1)} collective-permute-done((bf16[512,768]{1,0:T(8,128)(2,1)}, bf16[512,768]{1,0:T(8,128)(2,1)}, u32[]{:S(2)}, u32[]{:S(2)}) %collective-permute-start.11) | collective-permute-done | bytes 786464 | tf_op jit(solution)/shard_map/ppermute | solution.py:254
  151.8 4.0 %spread.1 = bf16[1024,768]{1,0:T(8,128)(2,1)} custom-call(bf16[1024,512]{1,0:T(8,128)(2,1)S(1)} %fusion.place_ref, f32[512,1]{1,0:T(8,128)S(1)} %copy.15.scale_ref, f32[512,768]{1,0:T(8,128)S(1)} %down.5.own_ref, bf16[512,768]{1,0:T(8,128)(2,1)} %collective-permute-done.11.right_ref, bf16[512,768]{1,0:T(8,128)(2,1)S(1)} %collective-permute-done.15.left_ref), custom_call_target="tpu_custom_call" | custom-call | tf_op jit(solution)/shard_map/spread/pallas_call | solution.py:223
  (21 shorter events, 0.3 us)
Async XLA Ops:
  0.7 1.4 copy-start
  3.5 20.5 %collective-permute-start = (bf16[512,768]{1,0:T(8,128)(2,1)S(1)}, bf16[512,768]{1,0:T(8,128)(2,1)S(1)}, u32[]{:S(2)}, u32[]{:S(2)}) collective-permute-start(bf16[512,768]{1,0:T(8,128)(2,1)S(1)} %get-tuple-element.24.refs_0_), channel_id=1, source_target_pairs={{0,2},{2,4},{4,6},{6,7},{7,5},{5,3},{3,1},{1,0},{8,10},{10,12},{12... | collective-permute-start | bytes 2359304 | tf_op jit(solution)/shard_map/ppermute | solution.py:254
  6.6 19.3 %collective-permute-start.4 = (bf16[512,768]{1,0:T(8,128)(2,1)S(1)}, bf16[512,768]{1,0:T(8,128)(2,1)S(1)}, u32[]{:S(2)}, u32[]{:S(2)}) collective-permute-start(bf16[512,768]{1,0:T(8,128)(2,1)S(1)} %get-tuple-element.24.refs_0_), channel_id=1, source_target_pairs={{2,0},{4,2},{6,4},{7,6},{5,7},{3,5},{1,3},{0,1},{10,8},{12,10},{14... | collective-permute-start | bytes 2359304 | tf_op jit(solution)/shard_map/ppermute | solution.py:257
  24.0 18.7 %collective-permute-start.1 = (bf16[512,768]{1,0:T(8,128)(2,1)S(1)}, bf16[512,768]{1,0:T(8,128)(2,1)S(1)}, u32[]{:S(2)}, u32[]{:S(2)}) collective-permute-start(bf16[512,768]{1,0:T(8,128)(2,1)S(1)} %collective-permute-done.refs_0_), channel_id=1, source_target_pairs={{0,2},{2,4},{4,6},{6,7},{7,5},{5,3},{3,1},{1,0},{8,10},{10,12},{12... | collective-permute-start | bytes 2359304 | tf_op jit(solution)/shard_map/ppermute | solution.py:254
  25.9 18.4 %collective-permute-start.5 = (bf16[512,768]{1,0:T(8,128)(2,1)S(1)}, bf16[512,768]{1,0:T(8,128)(2,1)S(1)}, u32[]{:S(2)}, u32[]{:S(2)}) collective-permute-start(bf16[512,768]{1,0:T(8,128)(2,1)S(1)} %collective-permute-done.4.refs_1_), channel_id=1, source_target_pairs={{2,0},{4,2},{6,4},{7,6},{5,7},{3,5},{1,3},{0,1},{10,8},{12,10},{14... | collective-permute-start | bytes 2359304 | tf_op jit(solution)/shard_map/ppermute | solution.py:257
  42.8 17.8 %collective-permute-start.2 = (bf16[512,768]{1,0:T(8,128)(2,1)S(1)}, bf16[512,768]{1,0:T(8,128)(2,1)S(1)}, u32[]{:S(2)}, u32[]{:S(2)}) collective-permute-start(bf16[512,768]{1,0:T(8,128)(2,1)S(1)} %collective-permute-done.1.refs_0_), channel_id=1, source_target_pairs={{0,2},{2,4},{4,6},{6,7},{7,5},{5,3},{3,1},{1,0},{8,10},{10,12},{12... | collective-permute-start | bytes 2359304 | tf_op jit(solution)/shard_map/ppermute | solution.py:254
  44.3 17.7 %collective-permute-start.6 = (bf16[512,768]{1,0:T(8,128)(2,1)S(1)}, bf16[512,768]{1,0:T(8,128)(2,1)S(1)}, u32[]{:S(2)}, u32[]{:S(2)}) collective-permute-start(bf16[512,768]{1,0:T(8,128)(2,1)S(1)} %collective-permute-done.5.refs_1_), channel_id=1, source_target_pairs={{2,0},{4,2},{6,4},{7,6},{5,7},{3,5},{1,3},{0,1},{10,8},{12,10},{14... | collective-permute-start | bytes 2359304 | tf_op jit(solution)/shard_map/ppermute | solution.py:257
  60.6 12.8 %collective-permute-start.3 = (bf16[256,768]{1,0:T(8,128)(2,1)S(1)}, bf16[256,768]{1,0:T(8,128)(2,1)S(1)}, u32[]{:S(2)}, u32[]{:S(2)}) collective-permute-start(bf16[256,768]{1,0:T(8,128)(2,1)S(1)} %slice.26), channel_id=1, source_target_pairs={{0,2},{2,4},{4,6},{6,7},{7,5},{5,3},{3,1},{1,0},{8,10},{10,12},{12... | collective-permute-start | bytes 1179656 | tf_op jit(solution)/shard_map/ppermute | solution.py:254
  62.0 11.4 %collective-permute-start.7 = (bf16[256,768]{1,0:T(8,128)(2,1)S(1)}, bf16[256,768]{1,0:T(8,128)(2,1)S(1)}, u32[]{:S(2)}, u32[]{:S(2)}) collective-permute-start(bf16[256,768]{1,0:T(8,128)(2,1)S(1)} %slice.27), channel_id=1, source_target_pairs={{2,0},{4,2},{6,4},{7,6},{5,7},{3,5},{1,3},{0,1},{10,8},{12,10},{14... | collective-permute-start | bytes 1179656 | tf_op jit(solution)/shard_map/ppermute | solution.py:257
  85.1 9.0 %collective-permute-start.12 = (bf16[256,768]{1,0:T(8,128)(2,1)S(1)}, bf16[256,768]{1,0:T(8,128)(2,1)S(1)}, u32[]{:S(2)}, u32[]{:S(2)}) collective-permute-start(bf16[256,768]{1,0:T(8,128)(2,1)S(1)} %get-tuple-element.40), channel_id=1, source_target_pairs={{2,0},{4,2},{6,4},{7,6},{5,7},{3,5},{1,3},{0,1},{10,8},{12,10},{14... | collective-permute-start | bytes 1179656 | tf_op jit(solution)/shard_map/ppermute | solution.py:257
  93.3 10.0 %collective-permute-start.8 = (bf16[256,768]{1,0:T(8,128)(2,1)S(1)}, bf16[256,768]{1,0:T(8,128)(2,1)S(1)}, u32[]{:S(2)}, u32[]{:S(2)}) collective-permute-start(bf16[256,768]{1,0:T(8,128)(2,1)S(1)} %get-tuple-element.36), channel_id=1, source_target_pairs={{0,2},{2,4},{4,6},{6,7},{7,5},{5,3},{3,1},{1,0},{8,10},{10,12},{12... | collective-permute-start | bytes 1179656 | tf_op jit(solution)/shard_map/ppermute | solution.py:254
  94.3 17.5 %collective-permute-start.13 = (bf16[512,768]{1,0:T(8,128)(2,1)S(1)}, bf16[512,768]{1,0:T(8,128)(2,1)S(1)}, u32[]{:S(2)}, u32[]{:S(2)}) collective-permute-start(bf16[512,768]{1,0:T(8,128)(2,1)S(1)} %pad_maximum_fusion.1), channel_id=1, source_target_pairs={{2,0},{4,2},{6,4},{7,6},{5,7},{3,5},{1,3},{0,1},{10,8},{12,10},{14... | collective-permute-start | bytes 2359304 | tf_op jit(solution)/shard_map/ppermute | solution.py:257
  103.4 17.3 %collective-permute-start.9 = (bf16[512,768]{1,0:T(8,128)(2,1)S(1)}, bf16[512,768]{1,0:T(8,128)(2,1)S(1)}, u32[]{:S(2)}, u32[]{:S(2)}) collective-permute-start(bf16[512,768]{1,0:T(8,128)(2,1)S(1)} %pad_maximum_fusion), channel_id=1, source_target_pairs={{0,2},{2,4},{4,6},{6,7},{7,5},{5,3},{3,1},{1,0},{8,10},{10,12},{12... | collective-permute-start | bytes 2359304 | tf_op jit(solution)/shard_map/ppermute | solution.py:254
  112.0 16.5 %collective-permute-start.14 = (bf16[512,768]{1,0:T(8,128)(2,1)S(1)}, bf16[512,768]{1,0:T(8,128)(2,1)S(1)}, u32[]{:S(2)}, u32[]{:S(2)}) collective-permute-start(bf16[512,768]{1,0:T(8,128)(2,1)S(1)} %add_convert_fusion.1), channel_id=1, source_target_pairs={{2,0},{4,2},{6,4},{7,6},{5,7},{3,5},{1,3},{0,1},{10,8},{12,10},{14... | collective-permute-start | bytes 2359304 | tf_op jit(solution)/shard_map/ppermute | solution.py:257
  120.9 16.7 %collective-permute-start.10 = (bf16[512,768]{1,0:T(8,128)(2,1)S(1)}, bf16[512,768]{1,0:T(8,128)(2,1)S(1)}, u32[]{:S(2)}, u32[]{:S(2)}) collective-permute-start(bf16[512,768]{1,0:T(8,128)(2,1)S(1)} %add_convert_fusion.3), channel_id=1, source_target_pairs={{0,2},{2,4},{4,6},{6,7},{7,5},{5,3},{3,1},{1,0},{8,10},{10,12},{12... | collective-permute-start | bytes 2359304 | tf_op jit(solution)/shard_map/ppermute | solution.py:254
  129.5 14.8 %collective-permute-start.15 = (bf16[512,768]{1,0:T(8,128)(2,1)}, bf16[512,768]{1,0:T(8,128)(2,1)S(1)}, u32[]{:S(2)}, u32[]{:S(2)}) collective-permute-start(bf16[512,768]{1,0:T(8,128)(2,1)} %add_convert_fusion), channel_id=1, source_target_pairs={{2,0},{4,2},{6,4},{7,6},{5,7},{3,5},{1,3},{0,1},{10,8},{12,10},{14... | collective-permute-start | bytes 2359304 | tf_op jit(solution)/shard_map/ppermute | solution.py:257
  137.6 1.4 copy-start.1
  137.6 1.4 copy-start.2
  138.7 13.1 %collective-permute-start.11 = (bf16[512,768]{1,0:T(8,128)(2,1)}, bf16[512,768]{1,0:T(8,128)(2,1)}, u32[]{:S(2)}, u32[]{:S(2)}) collective-permute-start(bf16[512,768]{1,0:T(8,128)(2,1)} %add_convert_fusion.2), channel_id=1, source_target_pairs={{0,2},{2,4},{4,6},{6,7},{7,5},{5,3},{3,1},{1,0},{8,10},{10,12},{12... | collective-permute-start | bytes 2359304 | tf_op jit(solution)/shard_map/ppermute | solution.py:254
where the time goes:
time: 156 us
  Pallas kernels  80.5 us (52%)
  waiting for transfers between devices  51.9 us (33%)
  starting transfers between devices  16.8 us (11%)
  other arithmetic  4.01 us (3%)
  local copies, waits for them, and re-layouts  2.39 us (2%)
    ppermute x8, waiting for transfers between devices, right_of(): return lax.ppermute(value, 'tensor', to_right)  50.5 us
    pallas_call x5, Pallas kernels, gate_up(): pl.pallas_call(functools.partial(gate_up_kernel, steps=steps, pieces=len(...  45.5 us
    pallas_call x5, Pallas kernels, down(): pl.pallas_call(functools.partial(down_kernel, steps=steps, split=split),...  29.6 us
    ppermute x8, starting transfers between devices, right_of(): return lax.ppermute(value, 'tensor', to_right)  9.84 us
    ppermute x8, starting transfers between devices, left_of(): return lax.ppermute(value, 'tensor', to_left)  6.91 us
    pallas_call x1, Pallas kernels, spread(): pl.pallas_call(spread_kernel, grid=(width // TILE,), in_specs=[pl.BlockSp...  4.01 us
  transfers between devices with their start and end apart: 16, of which 9 were waited for; matrix products, arithmetic and copies ran while one was open for 3% of the time, Pallas kernels for 41%

commit v1 on v0

--- a/solution.py
+++ b/solution.py
@@ -63,92 +63,156 @@
     return value / (1.0 + jnp.exp(-value))
 
 
-def gate_up_kernel(ids_ref, *refs, steps, pieces, first, last):
-    xs, refs = refs[:pieces], refs[pieces:]
+def gate_up_kernel(ids_ref, *refs, steps, first, fetch):
+    xs, refs = refs[: len(steps)], refs[len(steps) :]
     gate_weight, up_weight, *refs = refs
+    down_weight, refs = (refs[0], refs[1:]) if fetch is not None else (None, refs)
     gate_in, up_in = (None, None) if first else refs[:2]
     refs = refs if first else refs[2:]
-    hold, sem = refs[-2:]
+    gate_out, up_out, *refs = refs
+    hold, sem = refs[-2 if fetch is None else -4 :][:2]
     width = xs[0].shape[1]
     blocks, tile = hold.shape[0], hold.shape[-1]
 
-    def copy(n, which, j):
+    def copy(n, which, step, into, signal):
+        rows = pl.ds(pl.multiple_of(ids_ref[step] * width, width), width)
+        columns = pl.ds(pl.multiple_of(n * tile, tile), tile)
         weight = (gate_weight, up_weight)[which]
-        rows = pl.ds(pl.multiple_of(ids_ref[steps[j]] * width, width), width)
-        columns = pl.ds(pl.multiple_of(n * tile, tile), tile)
-        return pltpu.make_async_copy(
-            weight.at[rows, columns],
-            hold.at[n, which, j * width : (j + 1) * width],
-            sem.at[n, which, j],
-        )
+        return pltpu.make_async_copy(weight.at[rows, columns], into, signal)
+
+    def mine(n, which, j):
+        into = hold.at[n, which, j * width : (j + 1) * width]
+        return copy(n, which, steps[j], into, sem.at[n, which, j])
 
     def begin(n, carry):
         for which in range(2):
             for j in range(len(steps)):
-                copy(n, which, j).start()
+                mine(n, which, j).start()
         return carry
 
     def block(n, carry):
         at = pl.ds(pl.multiple_of(n * tile, tile), tile)
-        x = jnp.concatenate([piece[...] for piece in xs], axis=0 if last else 1)
-        values = []
+        x = jnp.concatenate([piece[...] for piece in xs], axis=1)
         for which in range(2):
             for j in range(len(steps)):
-                copy(n, which, j).wait()
+                mine(n, which, j).wait()
             value = dot(x, hold[n, which])
             if not first:
                 value = (gate_in, up_in)[which][:, at] + value
-            values.append(value)
-        if last:
-            refs[0][:, at] = (silu(values[0]) * values[1]).astype(BF16)
-        else:
-            refs[0][:, at], refs[1][:, at] = values
+            (gate_out, up_out)[which][:, at] = value
         return carry
 
     lax.fori_loop(0, blocks, begin, 0)
+    if fetch is None:
+        lax.fori_loop(0, blocks, block, 0)
+        return
+
+    next_ref, down_ref, _, _, next_sem, down_sem = refs
+    depth, breadth = down_ref.shape
+    columns = pl.ds(pl.multiple_of(ids_ref[fetch] * breadth, breadth), breadth)
+    below = pltpu.make_async_copy(down_weight.at[:, columns], down_ref, down_sem)
+
+    def ahead(n, which):
+        return copy(n, which, fetch, next_ref.at[n, which], next_sem.at[n, which])
+
+    def begin_ahead(n, carry):
+        for which in range(2):
+            ahead(n, which).start()
+        return carry
+
+    def end_ahead(n, carry):
+        for which in range(2):
+            ahead(n, which).wait()
+        return carry
+
+    lax.fori_loop(0, blocks, begin_ahead, 0)
+    below.start()
     lax.fori_loop(0, blocks, block, 0)
-
-
-def gate_up(ids, steps, xs, gate_weight, up_weight, sums, last=False):
-    width = xs[0].shape[1]
+    lax.fori_loop(0, blocks, end_ahead, 0)
+    below.wait()
+
+
+def gate_up(ids, steps, xs, gate_weight, up_weight, sums, down_weight=None, fetch=None):
+    slots, width = xs[0].shape
     hidden = gate_weight.shape[1]
-    slots = xs[0].shape[0] * (len(xs) if last else 1)
     first = sums is None
     on_chip = pl.BlockSpec(memory_space=pltpu.VMEM)
     away = pl.BlockSpec(memory_space=pl.ANY)
-    operands = [*xs, gate_weight, up_weight, *([] if first else sums)]
-    aliases = {}
-    if last:
-        out_shape, out_specs = jax.ShapeDtypeStruct((slots, hidden), BF16), on_chip
-    else:
-        out_shape = (pltpu.VMEM((slots, hidden), F32),) * 2
-        out_specs = (on_chip, on_chip)
-        if not first:
-            at = 1 + len(operands) - 2
-            aliases = {at: 0, at + 1: 1}
+    weights = [gate_weight, up_weight] + ([] if fetch is None else [down_weight])
+    operands = [*xs, *weights, *([] if first else sums)]
+    at = 1 + len(operands) - 2
     blocks = hidden // WIDE
+    out_shape = [pltpu.VMEM((slots, hidden), F32)] * 2
+    scratch = [
+        pltpu.VMEM((blocks, 2, width * len(steps), WIDE), BF16),
+        pltpu.SemaphoreType.DMA((blocks, 2, len(steps))),
+    ]
+    if fetch is not None:
+        out_shape += [pltpu.VMEM((blocks, 2, width, WIDE), BF16), pltpu.VMEM((hidden, width), BF16)]
+        scratch += [pltpu.SemaphoreType.DMA((blocks, 2)), pltpu.SemaphoreType.DMA]
     flops = 4 * slots * width * hidden * len(steps)
     moved = 4 * width * hidden * len(steps)
     return pl.pallas_call(
-        functools.partial(gate_up_kernel, steps=steps, pieces=len(xs), first=first, last=last),
+        functools.partial(gate_up_kernel, steps=steps, first=first, fetch=fetch),
         in_specs=[pl.BlockSpec(memory_space=pltpu.SMEM)]
         + [on_chip] * len(xs)
-        + [away] * 2
+        + [away] * len(weights)
         + [on_chip] * (0 if first else 2),
-        out_specs=out_specs,
+        out_specs=[on_chip] * len(out_shape),
         out_shape=out_shape,
-        scratch_shapes=[
-            pltpu.VMEM((blocks, 2, width * len(steps), WIDE), BF16),
-            pltpu.SemaphoreType.DMA((blocks, 2, len(steps))),
-        ],
-        input_output_aliases=aliases,
+        scratch_shapes=scratch,
+        input_output_aliases={} if first else {at: 0, at + 1: 1},
         compiler_params=params(),
         cost_estimate=pl.CostEstimate(flops=COST * flops, bytes_accessed=moved, transcendentals=0),
         name="gate_up",
     )(ids, *operands)
 
 
-def down_kernel(ids_ref, hidden_ref, weight_ref, *refs, steps, split):
+def turn_kernel(top_x, bottom_x, gate_in, up_in, next_ref, down_ref, hidden_ref, top_out, bottom_out):
+    blocks, tile = next_ref.shape[0], next_ref.shape[-1]
+    rows = top_out.shape[0]
+
+    def block(n, carry):
+        at = pl.ds(pl.multiple_of(n * tile, tile), tile)
+        x = jnp.concatenate([top_x[...], bottom_x[...]], axis=0)
+        gate = gate_in[:, at] + dot(x, next_ref[n, 0])
+        up = up_in[:, at] + dot(x, next_ref[n, 1])
+        hidden_ref[:, at] = (silu(gate) * up).astype(BF16)
+        return carry
+
+    def leave(n, carry):
+        at = pl.ds(pl.multiple_of(n * TILE, TILE), TILE)
+        value = dot(hidden_ref[...], down_ref[:, at])
+        top_out[:, at] = value[:rows].astype(BF16)
+        bottom_out[:, at] = value[rows:].astype(BF16)
+        return carry
+
+    lax.fori_loop(0, blocks, block, 0)
+    lax.fori_loop(0, down_ref.shape[1] // TILE, leave, 0)
+
+
+def turn(top, bottom, sums, next_weights, next_down):
+    rows, width = top.shape
+    hidden = sums[0].shape[1]
+    on_chip = pl.BlockSpec(memory_space=pltpu.VMEM)
+    return pl.pallas_call(
+        turn_kernel,
+        in_specs=[on_chip] * 6,
+        out_specs=[on_chip] * 3,
+        out_shape=[
+            pltpu.VMEM((2 * rows, hidden), BF16),
+            jax.ShapeDtypeStruct((rows, width), BF16),
+            jax.ShapeDtypeStruct((rows, width), BF16),
+        ],
+        compiler_params=params(),
+        cost_estimate=pl.CostEstimate(
+            flops=12 * rows * width * hidden, bytes_accessed=0, transcendentals=0
+        ),
+        name="turn",
+    )(top, bottom, *sums, next_weights, next_down)
+
+
+def down_kernel(ids_ref, hidden_ref, weight_ref, *refs, steps):
     outs, hold, sem = refs[:-2], *refs[-2:]
     width = hold.shape[-1]
     depth = hidden_ref.shape[1]
@@ -172,30 +236,20 @@
                     copy(i, k).wait()
 
             at = pl.ds(pl.multiple_of(n * TILE, TILE), TILE)
-            value = dot(hidden_ref[...], hold[i, :, at])
-            if split:
-                rows = outs[0].shape[0]
-                outs[0][:, at] = value[:rows].astype(BF16)
-                outs[1][:, at] = value[rows:].astype(BF16)
-            else:
-                outs[i][:, at] = value
+            outs[i][:, at] = dot(hidden_ref[...], hold[i, :, at])
             return carry
 
         lax.fori_loop(0, width // TILE, block, 0)
 
 
-def down(ids, steps, hidden, down_weight, width, split=False):
+def down(ids, steps, hidden, down_weight, width):
     slots, depth = hidden.shape
-    if split:
-        shape, kind, outs = (slots // 2, width), BF16, 2
-    else:
-        shape, kind, outs = (slots, width), F32, len(steps)
     on_chip = pl.BlockSpec(memory_space=pltpu.VMEM)
     return pl.pallas_call(
-        functools.partial(down_kernel, steps=steps, split=split),
+        functools.partial(down_kernel, steps=steps),
         in_specs=[pl.BlockSpec(memory_space=pltpu.SMEM), on_chip, pl.BlockSpec(memory_space=pl.ANY)],
-        out_specs=(on_chip,) * outs,
-        out_shape=(jax.ShapeDtypeStruct(shape, kind),) * outs,
+        out_specs=(on_chip,) * len(steps),
+        out_shape=(jax.ShapeDtypeStruct((slots, width), F32),) * len(steps),
         scratch_shapes=[
             pltpu.VMEM((len(steps), depth, width), BF16),
             pltpu.SemaphoreType.DMA((len(steps), 4)),
@@ -211,25 +265,18 @@
 
 
 def spread_kernel(place_ref, scale_ref, own_ref, right_ref, left_ref, out_ref):
-    total = own_ref[...] + right_ref[...].astype(F32) + left_ref[...].astype(F32)
-    scaled = (total * scale_ref[...]).astype(BF16)
-    out_ref[...] = dot(place_ref[...], scaled).astype(BF16)
+    at = pl.ds(pl.multiple_of(pl.program_id(0) * TILE, TILE), TILE)
+    total = own_ref[:, at] + right_ref[:, at].astype(F32) + left_ref[:, at].astype(F32)
+    out_ref[...] = dot(place_ref[...], (total * scale_ref[...]).astype(BF16)).astype(BF16)
 
 
 def spread(place, scale, own, right, left):
-    count, slots = place.shape
+    count = place.shape[0]
     width = own.shape[1]
-    block = pl.BlockSpec((slots, TILE), lambda n: (0, n))
     return pl.pallas_call(
         spread_kernel,
         grid=(width // TILE,),
-        in_specs=[
-            pl.BlockSpec(place.shape, lambda n: (0, 0)),
-            pl.BlockSpec(scale.shape, lambda n: (0, 0)),
-            block,
-            block,
-            block,
-        ],
+        in_specs=[pl.BlockSpec(memory_space=pltpu.VMEM)] * 5,
         out_specs=pl.BlockSpec((count, TILE), lambda n: (0, n)),
         out_shape=jax.ShapeDtypeStruct((count, width), BF16),
         compiler_params=params(),
@@ -256,6 +303,9 @@
     def left_of(value):
         return lax.ppermute(value, "tensor", to_left)
 
+    def both(one, other):
+        return lax.optimization_barrier((one, other))
+
     own, slot = compact(routed, tokens, slots)
 
     right, left = right_of(own), left_of(own)
@@ -266,11 +316,15 @@
             right, left = right_of(right), left_of(left)
         else:
             right, left = right_of(right[: slots // 2]), left_of(left[slots // 2 :])
-        sums = gate_up(ids, [size - s, s], here, gate_weight, up_weight, sums)
-    hidden = gate_up(ids, [half], [right, left], gate_weight, up_weight, sums, last=True)
-
-    top, bottom = down(ids, [half], hidden, down_weight, width, split=True)
-    right, left = right_of(top), left_of(bottom)
+        if s == max(1, half - 2):
+            *sums, next_weights, next_down = gate_up(
+                ids, [size - s, s], here, gate_weight, up_weight, sums, down_weight, fetch=half
+            )
+        else:
+            sums = gate_up(ids, [size - s, s], here, gate_weight, up_weight, sums)
+    hidden, top, bottom = turn(right, left, sums, next_weights, next_down)
+
+    right, left = both(right_of(top), left_of(bottom))
     for s in range(half - 1, 0, -1):
         ahead, behind = down(ids, [s, size - s], hidden, down_weight, width)
         if s == half - 1:
@@ -280,7 +334,7 @@
         else:
             ahead = ahead + right.astype(F32)
             behind = behind + left.astype(F32)
-        right, left = right_of(ahead.astype(BF16)), left_of(behind.astype(BF16))
+        right, left = both(right_of(ahead.astype(BF16)), left_of(behind.astype(BF16)))
     (mine,) = down(ids, [0], hidden, down_weight, width)
 
     slot = slot.reshape(-1)

time: 156 us -> 143 us (0.917)
  waiting for transfers between devices: 51.9 us -> 44.4 us
  Pallas kernels: 80.5 us -> 73.8 us
    ppermute x8, waiting for transfers between devices: 50.5 us -> 22.2 us  [right_of(): return lax.ppermute(value, 'tensor', to_right)]
    ppermute x8, waiting for transfers between devices: 1.46 us -> 22.2 us  [left_of(): return lax.ppermute(value, 'tensor', to_left)]
    pallas_call x10 -> x9, Pallas kernels: 75.1 us -> 68.6 us  [the longest x4 37.3 us: gate_up(): pl.pallas_call(functools.partial(gate_up_kernel, steps=steps, first=first...]
    ppermute x8, starting transfers between devices: 9.84 us -> 14.5 us  [right_of(): return lax.ppermute(value, 'tensor', to_right)]
    ppermute x8, starting transfers between devices: 6.91 us -> 3.61 us  [left_of(): return lax.ppermute(value, 'tensor', to_left)]
  transfers between devices with their start and end apart: 16 -> 16, of which waited for: 9 -> 7; matrix products, arithmetic and copies ran while one was open for 3% -> 2% of each run, Pallas kernels for 41% -> 44%
where the time goes in v1:
time: 143 us
  Pallas kernels  73.8 us (52%)
  waiting for transfers between devices  44.4 us (31%)
  starting transfers between devices  18.1 us (13%)
  other arithmetic  4.01 us (3%)
  local copies, waits for them, and re-layouts  2.39 us (2%)
    pallas_call x4, Pallas kernels, gate_up(): pl.pallas_call(functools.partial(gate_up_kernel, steps=steps, first=first...  37.3 us
    pallas_call x4, Pallas kernels, down(): pl.pallas_call(functools.partial(down_kernel, steps=steps), in_specs=[pl....  25 us
    ppermute x8, waiting for transfers between devices, left_of(): return lax.ppermute(value, 'tensor', to_left)  22.2 us
    ppermute x8, waiting for transfers between devices, right_of(): return lax.ppermute(value, 'tensor', to_right)  22.2 us
    ppermute x8, starting transfers between devices, right_of(): return lax.ppermute(value, 'tensor', to_right)  14.5 us
    pallas_call x1, Pallas kernels, turn(): pl.pallas_call(turn_kernel, in_specs=[on_chip] * 6, out_specs=[on_chip] *...  6.28 us
    pallas_call x1, Pallas kernels, spread(): pl.pallas_call(spread_kernel, grid=(width // TILE,), in_specs=[pl.BlockSp...  3.82 us
    ppermute x8, starting transfers between devices, left_of(): return lax.ppermute(value, 'tensor', to_left)  3.61 us
  transfers between devices with their start and end apart: 16, of which 7 were waited for; matrix products, arithmetic and copies ran while one was open for 2% of the time, Pallas kernels for 44%

profile of v1, /device:TPU:0, one launch (start us, length us, event | category | flops | bytes accessed | tf_op | source)
XLA Modules:
  0.0 142.9 jit_solution(8211945674012399915)
XLA Ops:
  0.0 0.7 fusion.1
  0.7 1.4 copy-done
  2.1 1.4 compact.1
  3.5 3.1 %collective-permute-start = (bf16[512,768]{1,0:T(8,128)(2,1)S(1)}, bf16[512,768]{1,0:T(8,128)(2,1)S(1)}, u32[]{:S(2)}, u32[]{:S(2)}) collective-permute-start(bf16[512,768]{1,0:T(8,128)(2,1)S(1)} %get-tuple-element.35.refs_0_), channel_id=1, source_target_pairs={{0,2},{2,4},{4,6},{6,7},{7,5},{5,3},{3,1},{1,0},{8,10},{10,12},{12... | collective-permute-start | bytes 2359304 | tf_op jit(solution)/shard_map/ppermute | solution.py:301
  6.6 0.7 dynamic-slice_bitcast_fusion.ids_ref
  7.3 6.5 %gate_up.4 = (f32[512,2048]{1,0:T(8,128)S(1)}, f32[512,2048]{1,0:T(8,128)S(1)}) custom-call(s32[8]{0:T(128)S(1)} %dynamic-slice_bitcast_fusion.ids_ref, bf16[512,768]{1,0:T(8,128)(2,1)S(1)} %get-tuple-element.35.refs_0_, bf16[6144,2048]{1,0:T(8,128)(2,1)} %refs_2_.7, bf16[6144,2048]{1,0:T(8,128)(2,1)} %refs_3_.5), custom_call_target="tpu_custom_call" | custom-call | flops 6442450944 | bytes 6291456 | tf_op jit(solution)/shard_map/gate_up/pallas_call | solution.py:155
  13.8 10.3 %collective-permute-done.refs_0_ = bf16[512,768]{1,0:T(8,128)(2,1)S(1)} collective-permute-done((bf16[512,768]{1,0:T(8,128)(2,1)S(1)}, bf16[512,768]{1,0:T(8,128)(2,1)S(1)}, u32[]{:S(2)}, u32[]{:S(2)}) %collective-permute-start) | collective-permute-done | bytes 786464 | tf_op jit(solution)/shard_map/ppermute | solution.py:301
  24.0 1.8 %collective-permute-start.1 = (bf16[512,768]{1,0:T(8,128)(2,1)S(1)}, bf16[512,768]{1,0:T(8,128)(2,1)S(1)}, u32[]{:S(2)}, u32[]{:S(2)}) collective-permute-start(bf16[512,768]{1,0:T(8,128)(2,1)S(1)} %collective-permute-done.refs_0_), channel_id=1, source_target_pairs={{0,2},{2,4},{4,6},{6,7},{7,5},{5,3},{3,1},{1,0},{8,10},{10,12},{12... | collective-permute-start | bytes 2359304 | tf_op jit(solution)/shard_map/ppermute | solution.py:301
  25.9 0.2 collective-permute-start.5
  26.1 10.2 %gate_up.5 = (f32[512,2048]{1,0:T(8,128)S(1)}, f32[512,2048]{1,0:T(8,128)S(1)}) custom-call(s32[8]{0:T(128)S(1)} %dynamic-slice_bitcast_fusion.ids_ref, bf16[512,768]{1,0:T(8,128)(2,1)S(1)} %collective-permute-done.refs_0_, bf16[512,768]{1,0:T(8,128)(2,1)S(1)} %collective-permute-done.4.refs_1_, ...), custom_call_target="tpu_custom_call", output_to_operand_aliasing={{0}: (5, {}), {1}: (6, {})} | custom-call | flops 12884901888 | bytes 12582912 | tf_op jit(solution)/shard_map/gate_up/pallas_call | solution.py:155
  36.3 6.5 %collective-permute-done.1.refs_0_ = bf16[512,768]{1,0:T(8,128)(2,1)S(1)} collective-permute-done((bf16[512,768]{1,0:T(8,128)(2,1)S(1)}, bf16[512,768]{1,0:T(8,128)(2,1)S(1)}, u32[]{:S(2)}, u32[]{:S(2)}) %collective-permute-start.1) | collective-permute-done | bytes 786464 | tf_op jit(solution)/shard_map/ppermute | solution.py:301
  42.8 1.5 %collective-permute-start.2 = (bf16[512,768]{1,0:T(8,128)(2,1)S(1)}, bf16[512,768]{1,0:T(8,128)(2,1)S(1)}, u32[]{:S(2)}, u32[]{:S(2)}) collective-permute-start(bf16[512,768]{1,0:T(8,128)(2,1)S(1)} %collective-permute-done.1.refs_0_), channel_id=1, source_target_pairs={{0,2},{2,4},{4,6},{6,7},{7,5},{5,3},{3,1},{1,0},{8,10},{10,12},{12... | collective-permute-start | bytes 2359304 | tf_op jit(solution)/shard_map/ppermute | solution.py:301
  44.3 0.5 collective-permute-start.6
  44.8 10.3 %gate_up.6 = (f32[512,2048]{1,0:T(8,128)S(1)}, f32[512,2048]{1,0:T(8,128)S(1)}, bf16[4,2,768,512]{3,2,1,0:T(8,128)(2,1)S(1)}, bf16[2048,768]{1,0:T(8,128)(2,1)S(1)}) custom-call(s32[8]{0:T(128)S(1)} %dynamic-slice_bitcast_fusion.ids_ref, bf16[512,768]{1,0:T(8,128)(2,1)S(1)} %collective-permute-done.1.refs_0_, ...), custom_call_target="tpu_custom_call", output_to_operand_aliasing={{0}: (6, {}), {1}: (7, {})} | custom-call | flops 12884901888 | bytes 12582912 | tf_op jit(solution)/shard_map/gate_up/pallas_call | solution.py:155
  55.2 5.4 %collective-permute-done.2.refs_0_ = bf16[512,768]{1,0:T(8,128)(2,1)S(1)} collective-permute-done((bf16[512,768]{1,0:T(8,128)(2,1)S(1)}, bf16[512,768]{1,0:T(8,128)(2,1)S(1)}, u32[]{:S(2)}, u32[]{:S(2)}) %collective-permute-start.2) | collective-permute-done | bytes 786464 | tf_op jit(solution)/shard_map/ppermute | solution.py:301
  60.6 1.4 collective-permute-start.3
  62.0 0.8 collective-permute-start.7
  62.8 10.2 %gate_up.7 = (f32[512,2048]{1,0:T(8,128)S(1)}, f32[512,2048]{1,0:T(8,128)S(1)}) custom-call(s32[8]{0:T(128)S(1)} %dynamic-slice_bitcast_fusion.ids_ref, bf16[512,768]{1,0:T(8,128)(2,1)S(1)} %collective-permute-done.2.refs_0_, bf16[512,768]{1,0:T(8,128)(2,1)S(1)} %collective-permute-done.6.refs_1_, ...), custom_call_target="tpu_custom_call", output_to_operand_aliasing={{0}: (5, {}), {1}: (6, {})} | custom-call | flops 12884901888 | bytes 12582912 | tf_op jit(solution)/shard_map/gate_up/pallas_call | solution.py:155
  73.0 6.3 %turn.1 = (bf16[512,2048]{1,0:T(8,128)(2,1)S(1)}, bf16[256,768]{1,0:T(8,128)(2,1)S(1)}, bf16[256,768]{1,0:T(8,128)(2,1)S(1)}) custom-call(bf16[256,768]{1,0:T(8,128)(2,1)S(1)} %collective-permute-done.3.top_x, bf16[256,768]{1,0:T(8,128)(2,1)S(1)} %collective-permute-done.7.bottom_x, f32[512,2048]{1,0:T(8,128)S(1)} %get-tuple-element.42.gate_in, ...), custom_call_target="tpu_custom_call" | custom-call | flops 4831838208 | tf_op jit(solution)/shard_map/turn/pallas_call | solution.py:198
  79.3 1.4 collective-permute-start.8
  80.7 0.7 collective-permute-start.9
  81.4 6.8 %down.7 = (f32[512,768]{1,0:T(8,128)S(1)}, f32[512,768]{1,0:T(8,128)S(1)}) custom-call(s32[8]{0:T(128)S(1)} %dynamic-slice_bitcast_fusion.ids_ref, bf16[512,2048]{1,0:T(8,128)(2,1)S(1)} %get-tuple-element.46.hidden_ref, bf16[2048,6144]{1,0:T(8,128)(2,1)} %weight_ref.7), custom_call_target="tpu_custom_call" | custom-call | flops 6442450944 | bytes 6291456 | tf_op jit(solution)/shard_map/down/pallas_call | solution.py:248
  88.3 1.1 collective-permute-done.9
  89.4 0.1 add_convert_fusion.4
  89.5 0.1 pad_maximum_fusion.1
  89.6 0.7 collective-permute-start.11
  90.3 0.1 add_convert_fusion.5
  90.3 0.1 pad_maximum_fusion
  90.4 1.7 %collective-permute-start.10 = (bf16[512,768]{1,0:T(8,128)(2,1)S(1)}, bf16[512,768]{1,0:T(8,128)(2,1)S(1)}, u32[]{:S(2)}, u32[]{:S(2)}) collective-permute-start(bf16[512,768]{1,0:T(8,128)(2,1)S(1)} %pad_maximum_fusion), channel_id=1, source_target_pairs={{0,2},{2,4},{4,6},{6,7},{7,5},{5,3},{3,1},{1,0},{8,10},{10,12},{12... | collective-permute-start | bytes 2359304 | tf_op jit(solution)/shard_map/ppermute | solution.py:301
  92.1 6.8 %down.6 = (f32[512,768]{1,0:T(8,128)S(1)}, f32[512,768]{1,0:T(8,128)S(1)}) custom-call(s32[8]{0:T(128)S(1)} %dynamic-slice_bitcast_fusion.ids_ref, bf16[512,2048]{1,0:T(8,128)(2,1)S(1)} %get-tuple-element.46.hidden_ref, bf16[2048,6144]{1,0:T(8,128)(2,1)} %weight_ref.7), custom_call_target="tpu_custom_call" | custom-call | flops 6442450944 | bytes 6291456 | tf_op jit(solution)/shard_map/down/pallas_call | solution.py:248
  98.9 8.4 %collective-permute-done.11 = bf16[512,768]{1,0:T(8,128)(2,1)S(1)} collective-permute-done((bf16[512,768]{1,0:T(8,128)(2,1)S(1)}, bf16[512,768]{1,0:T(8,128)(2,1)S(1)}, u32[]{:S(2)}, u32[]{:S(2)}) %collective-permute-start.11) | collective-permute-done | bytes 786464 | tf_op jit(solution)/shard_map/ppermute | solution.py:304
  107.4 0.2 add_convert_fusion.2
  107.6 0.4 collective-permute-start.13
  108.0 0.2 add_convert_fusion.3
  108.2 1.9 %collective-permute-start.12 = (bf16[512,768]{1,0:T(8,128)(2,1)S(1)}, bf16[512,768]{1,0:T(8,128)(2,1)S(1)}, u32[]{:S(2)}, u32[]{:S(2)}) collective-permute-start(bf16[512,768]{1,0:T(8,128)(2,1)S(1)} %add_convert_fusion.3), channel_id=1, source_target_pairs={{0,2},{2,4},{4,6},{6,7},{7,5},{5,3},{3,1},{1,0},{8,10},{10,12},{12... | collective-permute-start | bytes 2359304 | tf_op jit(solution)/shard_map/ppermute | solution.py:301
  110.1 6.8 %down.5 = (f32[512,768]{1,0:T(8,128)S(1)}, f32[512,768]{1,0:T(8,128)S(1)}) custom-call(s32[8]{0:T(128)S(1)} %dynamic-slice_bitcast_fusion.ids_ref, bf16[512,2048]{1,0:T(8,128)(2,1)S(1)} %get-tuple-element.46.hidden_ref, bf16[2048,6144]{1,0:T(8,128)(2,1)} %weight_ref.7), custom_call_target="tpu_custom_call" | custom-call | flops 6442450944 | bytes 6291456 | tf_op jit(solution)/shard_map/down/pallas_call | solution.py:248
  116.9 7.2 %collective-permute-done.13 = bf16[512,768]{1,0:T(8,128)(2,1)S(1)} collective-permute-done((bf16[512,768]{1,0:T(8,128)(2,1)S(1)}, bf16[512,768]{1,0:T(8,128)(2,1)S(1)}, u32[]{:S(2)}, u32[]{:S(2)}) %collective-permute-start.13) | collective-permute-done | bytes 786464 | tf_op jit(solution)/shard_map/ppermute | solution.py:304
  124.0 1.1 add_convert_fusion
  125.1 0.3 collective-permute-start.15
  125.5 1.0 add_convert_fusion.1
  126.5 1.7 %collective-permute-start.14 = (bf16[512,768]{1,0:T(8,128)(2,1)}, bf16[512,768]{1,0:T(8,128)(2,1)}, u32[]{:S(2)}, u32[]{:S(2)}) collective-permute-start(bf16[512,768]{1,0:T(8,128)(2,1)} %add_convert_fusion.1), channel_id=1, source_target_pairs={{0,2},{2,4},{4,6},{6,7},{7,5},{5,3},{3,1},{1,0},{8,10},{10,12},{12... | collective-permute-start | bytes 2359304 | tf_op jit(solution)/shard_map/ppermute | solution.py:301
  128.2 0.3 select_reduce_fusion
  128.5 0.1 copy.15.scale_ref
  128.7 0.2 fusion.place_ref
  128.9 4.6 %down.4.own_ref = f32[512,768]{1,0:T(8,128)S(1)} custom-call(s32[8]{0:T(128)S(1)} %dynamic-slice_bitcast_fusion.ids_ref, bf16[512,2048]{1,0:T(8,128)(2,1)S(1)} %get-tuple-element.46.hidden_ref, bf16[2048,6144]{1,0:T(8,128)(2,1)} %weight_ref.7), custom_call_target="tpu_custom_call" | custom-call | flops 3221225472 | bytes 3145728 | tf_op jit(solution)/shard_map/down/pallas_call | solution.py:248
  133.5 5.5 %collective-permute-done.15.left_ref = bf16[512,768]{1,0:T(8,128)(2,1)S(1)} collective-permute-done((bf16[512,768]{1,0:T(8,128)(2,1)}, bf16[512,768]{1,0:T(8,128)(2,1)S(1)}, u32[]{:S(2)}, u32[]{:S(2)}) %collective-permute-start.15) | collective-permute-done | bytes 786464 | tf_op jit(solution)/shard_map/ppermute | solution.py:304
  139.0 0.0 collective-permute-done.14.right_ref
  139.1 3.8 %spread.1 = bf16[1024,768]{1,0:T(8,128)(2,1)} custom-call(bf16[1024,512]{1,0:T(8,128)(2,1)S(1)} %fusion.place_ref, f32[512,1]{1,0:T(8,128)S(1)} %copy.15.scale_ref, f32[512,768]{1,0:T(8,128)S(1)} %down.4.own_ref, bf16[512,768]{1,0:T(8,128)(2,1)} %collective-permute-done.14.right_ref, bf16[512,768]{1,0:T(8,128)(2,1)S(1)} %collective-permute-done.15.left_ref), custom_call_target="tpu_custom_call" | custom-call | tf_op jit(solution)/shard_map/spread/pallas_call | solution.py:276
  (20 shorter events, 0.2 us)
Async XLA Ops:
  0.7 1.4 copy-start
  3.5 20.5 %collective-permute-start = (bf16[512,768]{1,0:T(8,128)(2,1)S(1)}, bf16[512,768]{1,0:T(8,128)(2,1)S(1)}, u32[]{:S(2)}, u32[]{:S(2)}) collective-permute-start(bf16[512,768]{1,0:T(8,128)(2,1)S(1)} %get-tuple-element.35.refs_0_), channel_id=1, source_target_pairs={{0,2},{2,4},{4,6},{6,7},{7,5},{5,3},{3,1},{1,0},{8,10},{10,12},{12... | collective-permute-start | bytes 2359304 | tf_op jit(solution)/shard_map/ppermute | solution.py:301
  6.6 19.3 %collective-permute-start.4 = (bf16[512,768]{1,0:T(8,128)(2,1)S(1)}, bf16[512,768]{1,0:T(8,128)(2,1)S(1)}, u32[]{:S(2)}, u32[]{:S(2)}) collective-permute-start(bf16[512,768]{1,0:T(8,128)(2,1)S(1)} %get-tuple-element.35.refs_0_), channel_id=1, source_target_pairs={{2,0},{4,2},{6,4},{7,6},{5,7},{3,5},{1,3},{0,1},{10,8},{12,10},{14... | collective-permute-start | bytes 2359304 | tf_op jit(solution)/shard_map/ppermute | solution.py:304
  24.0 18.7 %collective-permute-start.1 = (bf16[512,768]{1,0:T(8,128)(2,1)S(1)}, bf16[512,768]{1,0:T(8,128)(2,1)S(1)}, u32[]{:S(2)}, u32[]{:S(2)}) collective-permute-start(bf16[512,768]{1,0:T(8,128)(2,1)S(1)} %collective-permute-done.refs_0_), channel_id=1, source_target_pairs={{0,2},{2,4},{4,6},{6,7},{7,5},{5,3},{3,1},{1,0},{8,10},{10,12},{12... | collective-permute-start | bytes 2359304 | tf_op jit(solution)/shard_map/ppermute | solution.py:301
  25.9 18.4 %collective-permute-start.5 = (bf16[512,768]{1,0:T(8,128)(2,1)S(1)}, bf16[512,768]{1,0:T(8,128)(2,1)S(1)}, u32[]{:S(2)}, u32[]{:S(2)}) collective-permute-start(bf16[512,768]{1,0:T(8,128)(2,1)S(1)} %collective-permute-done.4.refs_1_), channel_id=1, source_target_pairs={{2,0},{4,2},{6,4},{7,6},{5,7},{3,5},{1,3},{0,1},{10,8},{12,10},{14... | collective-permute-start | bytes 2359304 | tf_op jit(solution)/shard_map/ppermute | solution.py:304
  42.8 17.8 %collective-permute-start.2 = (bf16[512,768]{1,0:T(8,128)(2,1)S(1)}, bf16[512,768]{1,0:T(8,128)(2,1)S(1)}, u32[]{:S(2)}, u32[]{:S(2)}) collective-permute-start(bf16[512,768]{1,0:T(8,128)(2,1)S(1)} %collective-permute-done.1.refs_0_), channel_id=1, source_target_pairs={{0,2},{2,4},{4,6},{6,7},{7,5},{5,3},{3,1},{1,0},{8,10},{10,12},{12... | collective-permute-start | bytes 2359304 | tf_op jit(solution)/shard_map/ppermute | solution.py:301
  44.3 17.7 %collective-permute-start.6 = (bf16[512,768]{1,0:T(8,128)(2,1)S(1)}, bf16[512,768]{1,0:T(8,128)(2,1)S(1)}, u32[]{:S(2)}, u32[]{:S(2)}) collective-permute-start(bf16[512,768]{1,0:T(8,128)(2,1)S(1)} %collective-permute-done.5.refs_1_), channel_id=1, source_target_pairs={{2,0},{4,2},{6,4},{7,6},{5,7},{3,5},{1,3},{0,1},{10,8},{12,10},{14... | collective-permute-start | bytes 2359304 | tf_op jit(solution)/shard_map/ppermute | solution.py:304
  60.6 12.4 %collective-permute-start.3 = (bf16[256,768]{1,0:T(8,128)(2,1)S(1)}, bf16[256,768]{1,0:T(8,128)(2,1)S(1)}, u32[]{:S(2)}, u32[]{:S(2)}) collective-permute-start(bf16[256,768]{1,0:T(8,128)(2,1)S(1)} %slice.26), channel_id=1, source_target_pairs={{0,2},{2,4},{4,6},{6,7},{7,5},{5,3},{3,1},{1,0},{8,10},{10,12},{12... | collective-permute-start | bytes 1179656 | tf_op jit(solution)/shard_map/ppermute | solution.py:301
  62.0 11.0 %collective-permute-start.7 = (bf16[256,768]{1,0:T(8,128)(2,1)S(1)}, bf16[256,768]{1,0:T(8,128)(2,1)S(1)}, u32[]{:S(2)}, u32[]{:S(2)}) collective-permute-start(bf16[256,768]{1,0:T(8,128)(2,1)S(1)} %slice.27), channel_id=1, source_target_pairs={{2,0},{4,2},{6,4},{7,6},{5,7},{3,5},{1,3},{0,1},{10,8},{12,10},{14... | collective-permute-start | bytes 1179656 | tf_op jit(solution)/shard_map/ppermute | solution.py:304
  79.3 9.0 %collective-permute-start.8 = (bf16[256,768]{1,0:T(8,128)(2,1)S(1)}, bf16[256,768]{1,0:T(8,128)(2,1)S(1)}, u32[]{:S(2)}, u32[]{:S(2)}) collective-permute-start(bf16[256,768]{1,0:T(8,128)(2,1)S(1)} %get-tuple-element.50), channel_id=1, source_target_pairs={{0,2},{2,4},{4,6},{6,7},{7,5},{5,3},{3,1},{1,0},{8,10},{10,12},{12... | collective-permute-start | bytes 1179656 | tf_op jit(solution)/shard_map/ppermute | solution.py:301
  80.7 8.7 %collective-permute-start.9 = (bf16[256,768]{1,0:T(8,128)(2,1)S(1)}, bf16[256,768]{1,0:T(8,128)(2,1)S(1)}, u32[]{:S(2)}, u32[]{:S(2)}) collective-permute-start(bf16[256,768]{1,0:T(8,128)(2,1)S(1)} %get-tuple-element.51), channel_id=1, source_target_pairs={{2,0},{4,2},{6,4},{7,6},{5,7},{3,5},{1,3},{0,1},{10,8},{12,10},{14... | collective-permute-start | bytes 1179656 | tf_op jit(solution)/shard_map/ppermute | solution.py:304
  89.6 17.8 %collective-permute-start.11 = (bf16[512,768]{1,0:T(8,128)(2,1)S(1)}, bf16[512,768]{1,0:T(8,128)(2,1)S(1)}, u32[]{:S(2)}, u32[]{:S(2)}) collective-permute-start(bf16[512,768]{1,0:T(8,128)(2,1)S(1)} %pad_maximum_fusion.1), channel_id=1, source_target_pairs={{2,0},{4,2},{6,4},{7,6},{5,7},{3,5},{1,3},{0,1},{10,8},{12,10},{14... | collective-permute-start | bytes 2359304 | tf_op jit(solution)/shard_map/ppermute | solution.py:304
  90.4 17.0 %collective-permute-start.10 = (bf16[512,768]{1,0:T(8,128)(2,1)S(1)}, bf16[512,768]{1,0:T(8,128)(2,1)S(1)}, u32[]{:S(2)}, u32[]{:S(2)}) collective-permute-start(bf16[512,768]{1,0:T(8,128)(2,1)S(1)} %pad_maximum_fusion), channel_id=1, source_target_pairs={{0,2},{2,4},{4,6},{6,7},{7,5},{5,3},{3,1},{1,0},{8,10},{10,12},{12... | collective-permute-start | bytes 2359304 | tf_op jit(solution)/shard_map/ppermute | solution.py:301
  107.6 16.5 %collective-permute-start.13 = (bf16[512,768]{1,0:T(8,128)(2,1)S(1)}, bf16[512,768]{1,0:T(8,128)(2,1)S(1)}, u32[]{:S(2)}, u32[]{:S(2)}) collective-permute-start(bf16[512,768]{1,0:T(8,128)(2,1)S(1)} %add_convert_fusion.2), channel_id=1, source_target_pairs={{2,0},{4,2},{6,4},{7,6},{5,7},{3,5},{1,3},{0,1},{10,8},{12,10},{14... | collective-permute-start | bytes 2359304 | tf_op jit(solution)/shard_map/ppermute | solution.py:304
  108.2 15.9 %collective-permute-start.12 = (bf16[512,768]{1,0:T(8,128)(2,1)S(1)}, bf16[512,768]{1,0:T(8,128)(2,1)S(1)}, u32[]{:S(2)}, u32[]{:S(2)}) collective-permute-start(bf16[512,768]{1,0:T(8,128)(2,1)S(1)} %add_convert_fusion.3), channel_id=1, source_target_pairs={{0,2},{2,4},{4,6},{6,7},{7,5},{5,3},{3,1},{1,0},{8,10},{10,12},{12... | collective-permute-start | bytes 2359304 | tf_op jit(solution)/shard_map/ppermute | solution.py:301
  125.1 13.9 %collective-permute-start.15 = (bf16[512,768]{1,0:T(8,128)(2,1)}, bf16[512,768]{1,0:T(8,128)(2,1)S(1)}, u32[]{:S(2)}, u32[]{:S(2)}) collective-permute-start(bf16[512,768]{1,0:T(8,128)(2,1)} %add_convert_fusion), channel_id=1, source_target_pairs={{2,0},{4,2},{6,4},{7,6},{5,7},{3,5},{1,3},{0,1},{10,8},{12,10},{14... | collective-permute-start | bytes 2359304 | tf_op jit(solution)/shard_map/ppermute | solution.py:304
  125.5 2.7 %copy-start.1 = (s32[1024,2]{0,1:T(2,128)S(1)}, s32[1024,2]{0,1:T(2,128)}, u32[]{:S(2)}) copy-start(s32[1024,2]{0,1:T(2,128)} %param.8) | copy-start | bytes 24580
  125.5 2.7 %copy-start.2 = (f32[1024,2]{0,1:T(2,128)S(1)}, f32[1024,2]{0,1:T(2,128)}, u32[]{:S(2)}) copy-start(f32[1024,2]{0,1:T(2,128)} %param.9) | copy-start | bytes 24580
  126.5 12.5 %collective-permute-start.14 = (bf16[512,768]{1,0:T(8,128)(2,1)}, bf16[512,768]{1,0:T(8,128)(2,1)}, u32[]{:S(2)}, u32[]{:S(2)}) collective-permute-start(bf16[512,768]{1,0:T(8,128)(2,1)} %add_convert_fusion.1), channel_id=1, source_target_pairs={{0,2},{2,4},{4,6},{6,7},{7,5},{5,3},{3,1},{1,0},{8,10},{10,12},{12... | collective-permute-start | bytes 2359304 | tf_op jit(solution)/shard_map/ppermute | solution.py:301

commit v2 on v1

--- a/solution.py
+++ b/solution.py
@@ -12,6 +12,7 @@
 TILE = 256
 WIDE = 512
 COST = 2
+AHEAD = 4
 F32 = jnp.float32
 BF16 = jnp.bfloat16
 VMEM_BYTES = 28 * 1024 * 1024
@@ -25,10 +26,20 @@
     return jnp.dot(a, b, preferred_element_type=F32)
 
 
-def compact_kernel(routed_ref, tokens_ref, chosen_ref, slot_ref, select_ref):
-    slots = select_ref.shape[0]
-    groups = routed_ref.shape[0]
-    routed = routed_ref[...]
+def compact_kernel(named_ref, tokens_ref, chosen_ref, slot_ref, select_ref, held_ref, sem):
+    slots, count = select_ref.shape
+    groups = count // LANES
+    cuts = sem.shape[0]
+    deep = count // cuts
+
+    def bring(k):
+        rows = slice(k * deep, (k + 1) * deep)
+        return pltpu.make_async_copy(tokens_ref.at[rows], held_ref.at[rows], sem.at[k])
+
+    for k in range(cuts):
+        bring(k).start()
+    hits = jnp.max(jnp.where(named_ref[...] == 0, 1.0, 0.0), axis=0, keepdims=True)
+    routed = jnp.concatenate([hits[:, g * LANES : (g + 1) * LANES] for g in range(groups)], axis=0)
     above = lax.broadcasted_iota(jnp.int32, (LANES, LANES), 0) <= lax.broadcasted_iota(
         jnp.int32, (LANES, LANES), 1
     )
@@ -41,10 +52,12 @@
         slot = jnp.where(routed[g : g + 1, :] > 0, row.astype(jnp.int32) - 1, -1)
         slot_ref[g : g + 1, :] = slot
         select_ref[:, g * LANES : (g + 1) * LANES] = jnp.where(slot_ids == slot, 1.0, 0.0).astype(BF16)
-    chosen_ref[...] = dot(select_ref[...], tokens_ref[...]).astype(BF16)
-
-
-def compact(routed, tokens, slots):
+    for k in range(cuts):
+        bring(k).wait()
+    chosen_ref[...] = dot(select_ref[...], held_ref[...]).astype(BF16)
+
+
+def compact(expert_index, tokens, slots):
     count, width = tokens.shape
     groups = count // LANES
     return pl.pallas_call(
@@ -53,10 +66,15 @@
             jax.ShapeDtypeStruct((slots, width), BF16),
             jax.ShapeDtypeStruct((groups, LANES), jnp.int32),
         ),
-        scratch_shapes=[pltpu.VMEM((slots, count), BF16)],
+        in_specs=[pl.BlockSpec(memory_space=pltpu.VMEM), pl.BlockSpec(memory_space=pl.ANY)],
+        scratch_shapes=[
+            pltpu.VMEM((slots, count), BF16),
+            pltpu.VMEM((count, width), BF16),
+            pltpu.SemaphoreType.DMA((4,)),
+        ],
         compiler_params=params(),
         name="compact",
-    )(routed.astype(F32).reshape(groups, LANES), tokens)
+    )(expert_index.T, pltpu.with_memory_space_constraint(tokens, pltpu.HBM))
 
 
 def silu(value):
@@ -84,13 +102,20 @@
         into = hold.at[n, which, j * width : (j + 1) * width]
         return copy(n, which, steps[j], into, sem.at[n, which, j])
 
-    def begin(n, carry):
+    def begin(n):
         for which in range(2):
             for j in range(len(steps)):
                 mine(n, which, j).start()
-        return carry
 
     def block(n, carry):
+        @pl.when(n + AHEAD < blocks)
+        def _():
+            begin(n + AHEAD)
+
+        @pl.when(n == min(1, blocks - 1))
+        def _():
+            begin_ahead()
+
         at = pl.ds(pl.multiple_of(n * tile, tile), tile)
         x = jnp.concatenate([piece[...] for piece in xs], axis=1)
         for which in range(2):
@@ -102,34 +127,30 @@
             (gate_out, up_out)[which][:, at] = value
         return carry
 
-    lax.fori_loop(0, blocks, begin, 0)
-    if fetch is None:
-        lax.fori_loop(0, blocks, block, 0)
-        return
-
-    next_ref, down_ref, _, _, next_sem, down_sem = refs
-    depth, breadth = down_ref.shape
-    columns = pl.ds(pl.multiple_of(ids_ref[fetch] * breadth, breadth), breadth)
-    below = pltpu.make_async_copy(down_weight.at[:, columns], down_ref, down_sem)
+    if fetch is not None:
+        next_ref, down_ref, _, _, next_sem, down_sem = refs
+        depth, breadth = down_ref.shape
+        columns = pl.ds(pl.multiple_of(ids_ref[fetch] * breadth, breadth), breadth)
+        below = pltpu.make_async_copy(down_weight.at[:, columns], down_ref, down_sem)
 
     def ahead(n, which):
         return copy(n, which, fetch, next_ref.at[n, which], next_sem.at[n, which])
 
-    def begin_ahead(n, carry):
-        for which in range(2):
-            ahead(n, which).start()
-        return carry
-
-    def end_ahead(n, carry):
-        for which in range(2):
-            ahead(n, which).wait()
-        return carry
-
-    lax.fori_loop(0, blocks, begin_ahead, 0)
-    below.start()
+    def begin_ahead():
+        if fetch is not None:
+            for n in range(blocks):
+                for which in range(2):
+                    ahead(n, which).start()
+            below.start()
+
+    for n in range(min(AHEAD, blocks)):
+        begin(n)
     lax.fori_loop(0, blocks, block, 0)
-    lax.fori_loop(0, blocks, end_ahead, 0)
-    below.wait()
+    if fetch is not None:
+        for n in range(blocks):
+            for which in range(2):
+                ahead(n, which).wait()
+        below.wait()
 
 
 def gate_up(ids, steps, xs, gate_weight, up_weight, sums, down_weight=None, fetch=None):
@@ -187,8 +208,8 @@
         bottom_out[:, at] = value[rows:].astype(BF16)
         return carry
 
-    lax.fori_loop(0, blocks, block, 0)
-    lax.fori_loop(0, down_ref.shape[1] // TILE, leave, 0)
+    lax.fori_loop(0, blocks, block, 0, unroll=True)
+    lax.fori_loop(0, down_ref.shape[1] // TILE, leave, 0, unroll=True)
 
 
 def turn(top, bottom, sums, next_weights, next_down):
@@ -224,9 +245,8 @@
         rows = slice(k * deep, (k + 1) * deep)
         return pltpu.make_async_copy(weight_ref.at[rows, columns], hold.at[i, rows], sem.at[i, k])
 
-    for i in range(len(steps)):
-        for k in range(cuts):
-            copy(i, k).start()
+    for k in range(cuts):
+        copy(0, k).start()
     for i in range(len(steps)):
 
         def block(n, carry, i=i):
@@ -234,6 +254,8 @@
             def _():
                 for k in range(cuts):
                     copy(i, k).wait()
+                    if i + 1 < len(steps):
+                        copy(i + 1, k).start()
 
             at = pl.ds(pl.multiple_of(n * TILE, TILE), TILE)
             outs[i][:, at] = dot(hidden_ref[...], hold[i, :, at])
@@ -264,31 +286,11 @@
     )(ids, hidden, down_weight)
 
 
-def spread_kernel(place_ref, scale_ref, own_ref, right_ref, left_ref, out_ref):
-    at = pl.ds(pl.multiple_of(pl.program_id(0) * TILE, TILE), TILE)
-    total = own_ref[:, at] + right_ref[:, at].astype(F32) + left_ref[:, at].astype(F32)
-    out_ref[...] = dot(place_ref[...], (total * scale_ref[...]).astype(BF16)).astype(BF16)
-
-
-def spread(place, scale, own, right, left):
-    count = place.shape[0]
-    width = own.shape[1]
-    return pl.pallas_call(
-        spread_kernel,
-        grid=(width // TILE,),
-        in_specs=[pl.BlockSpec(memory_space=pltpu.VMEM)] * 5,
-        out_specs=pl.BlockSpec((count, TILE), lambda n: (0, n)),
-        out_shape=jax.ShapeDtypeStruct((count, width), BF16),
-        compiler_params=params(),
-        name="spread",
-    )(place, scale, own, right, left)
-
-
 def ring_of(size):
     return [*range(0, size, 2), *range(size - 1, 0, -2)]
 
 
-def ring_plan(size, slots, tokens, routed, factor, gate_weight, up_weight, down_weight):
+def ring_plan(size, slots, tokens, expert_index, factor, gate_weight, up_weight, down_weight):
     width = tokens.shape[1]
     half = size // 2
     order = ring_of(size)
@@ -306,7 +308,7 @@
     def both(one, other):
         return lax.optimization_barrier((one, other))
 
-    own, slot = compact(routed, tokens, slots)
+    own, slot = compact(expert_index, tokens, slots)
 
     right, left = right_of(own), left_of(own)
     sums = gate_up(ids, [0], [own], gate_weight, up_weight, None)
@@ -341,7 +343,8 @@
     slot_ids = jnp.arange(slots, dtype=jnp.int32)
     place = (slot[:, None] == slot_ids[None, :]).astype(BF16)
     scale = jnp.sum(jnp.where(slot_ids[:, None] == slot[None, :], factor[None, :], 0.0), axis=1)
-    return spread(place, scale[:, None], mine, right, left)
+    total = mine + right.astype(F32) + left.astype(F32)
+    return dot(place, (total * scale[:, None]).astype(BF16)).astype(BF16)
 
 
 def plain_plan(slots, tokens, routed, factor, gate_weight, up_weight, down_weight):
@@ -362,7 +365,7 @@
     chosen = expert_index == 0
     routed = jnp.any(chosen, axis=1)
     factor = jnp.sum(jnp.where(chosen, combine_weight, 0.0), axis=1)
-    rest = (tokens, routed, factor, gate_weight, up_weight, down_weight)
+    weights = (gate_weight, up_weight, down_weight)
     fits = (
         size >= 4
         and size % 2 == 0
@@ -371,8 +374,8 @@
         and tokens.shape[0] % LANES == 0
     )
     if not fits:
-        return plain_plan(MOST, *rest)
-    return ring_plan(size, MOST, *rest)
+        return plain_plan(MOST, tokens, routed, factor, *weights)
+    return ring_plan(size, MOST, tokens, expert_index, factor, *weights)
 
 
 def solution(mesh):

time: 143 us -> 141 us (0.986)
  Pallas kernels: 73.8 us -> 70.4 us
  other arithmetic: 4.01 us -> 1.24 us
  matrix products: 0 us -> 2.47 us
  waiting for transfers between devices: 44.4 us -> 46.5 us
    pallas_call x1 -> x0, Pallas kernels: 3.82 us -> none  [spread(): pl.pallas_call(spread_kernel, grid=(width // TILE,), in_specs=[pl.BlockSp...]
    dot_general x0 -> x1, matrix products: none -> 2.47 us  [dot(): return jnp.dot(a, b, preferred_element_type=F32)]
    ppermute x8, waiting for transfers between devices: 22.2 us -> 24.4 us  [left_of(): return lax.ppermute(value, 'tensor', to_left)]
  transfers between devices with their start and end apart: 16 -> 16, of which waited for: 7 -> 7; matrix products, arithmetic and copies ran while one was open for 2% -> 1% of each run, Pallas kernels for 44% -> 45%
where the time goes in v2:
time: 141 us; the launch traced here: 140 us
  Pallas kernels  70.4 us (50%)
  waiting for transfers between devices  46.5 us (33%)
  starting transfers between devices  18 us (13%)
  matrix products  2.47 us (2%)
  local copies, waits for them, and re-layouts  1.53 us (1%)
    pallas_call x4, Pallas kernels, gate_up(): pl.pallas_call(functools.partial(gate_up_kernel, steps=steps, first=first...  37.4 us
    pallas_call x4, Pallas kernels, down(): pl.pallas_call(functools.partial(down_kernel, steps=steps), in_specs=[pl....  25.2 us
    ppermute x8, waiting for transfers between devices, left_of(): return lax.ppermute(value, 'tensor', to_left)  24.4 us
    ppermute x8, waiting for transfers between devices, right_of(): return lax.ppermute(value, 'tensor', to_right)  22.1 us
    ppermute x8, starting transfers between devices, right_of(): return lax.ppermute(value, 'tensor', to_right)  14.4 us
    pallas_call x1, Pallas kernels, turn(): pl.pallas_call(turn_kernel, in_specs=[on_chip] * 6, out_specs=[on_chip] *...  5.54 us
    ppermute x8, starting transfers between devices, left_of(): return lax.ppermute(value, 'tensor', to_left)  3.63 us
  transfers between devices with their start and end apart: 16, of which 7 were waited for; matrix products, arithmetic and copies ran while one was open for 1% of the time, Pallas kernels for 45%

profile of v2, /device:TPU:0, one launch (start us, length us, event | category | flops | bytes accessed | tf_op | source)
XLA Modules:
  0.0 140.4 jit_solution(12746423002225892136)
XLA Ops:
  0.0 0.7 copy-done
  0.7 2.4 %compact.1 = (bf16[512,768]{1,0:T(8,128)(2,1)S(1)}, s32[8,128]{1,0:T(8,128)S(1)}) custom-call(s32[2,1024]{1,0:T(2,128)S(1)} %bitcast.4, bf16[1024,768]{1,0:T(8,128)(2,1)} %tokens_ref.1), custom_call_target="tpu_custom_call" | custom-call | tf_op jit(solution)/shard_map/compact/pallas_call | solution.py:63
  3.1 3.1 %collective-permute-start = (bf16[512,768]{1,0:T(8,128)(2,1)S(1)}, bf16[512,768]{1,0:T(8,128)(2,1)S(1)}, u32[]{:S(2)}, u32[]{:S(2)}) collective-permute-start(bf16[512,768]{1,0:T(8,128)(2,1)S(1)} %get-tuple-element.35.refs_0_), channel_id=1, source_target_pairs={{0,2},{2,4},{4,6},{6,7},{7,5},{5,3},{3,1},{1,0},{8,10},{10,12},{12... | collective-permute-start | bytes 2359304 | tf_op jit(solution)/shard_map/ppermute | solution.py:303
  6.2 0.0 collective-permute-start.4
  6.2 0.7 dynamic-slice_bitcast_fusion.ids_ref
  6.9 6.5 %gate_up.4 = (f32[512,2048]{1,0:T(8,128)S(1)}, f32[512,2048]{1,0:T(8,128)S(1)}) custom-call(s32[8]{0:T(128)S(1)} %dynamic-slice_bitcast_fusion.ids_ref, bf16[512,768]{1,0:T(8,128)(2,1)S(1)} %get-tuple-element.35.refs_0_, bf16[6144,2048]{1,0:T(8,128)(2,1)} %refs_2_.7, bf16[6144,2048]{1,0:T(8,128)(2,1)} %refs_3_.5), custom_call_target="tpu_custom_call" | custom-call | flops 6442450944 | bytes 6291456 | tf_op jit(solution)/shard_map/gate_up/pallas_call | solution.py:176
  13.3 10.3 %collective-permute-done.refs_0_ = bf16[512,768]{1,0:T(8,128)(2,1)S(1)} collective-permute-done((bf16[512,768]{1,0:T(8,128)(2,1)S(1)}, bf16[512,768]{1,0:T(8,128)(2,1)S(1)}, u32[]{:S(2)}, u32[]{:S(2)}) %collective-permute-start) | collective-permute-done | bytes 786464 | tf_op jit(solution)/shard_map/ppermute | solution.py:303
  23.6 1.8 %collective-permute-start.1 = (bf16[512,768]{1,0:T(8,128)(2,1)S(1)}, bf16[512,768]{1,0:T(8,128)(2,1)S(1)}, u32[]{:S(2)}, u32[]{:S(2)}) collective-permute-start(bf16[512,768]{1,0:T(8,128)(2,1)S(1)} %collective-permute-done.refs_0_), channel_id=1, source_target_pairs={{0,2},{2,4},{4,6},{6,7},{7,5},{5,3},{3,1},{1,0},{8,10},{10,12},{12... | collective-permute-start | bytes 2359304 | tf_op jit(solution)/shard_map/ppermute | solution.py:303
  25.4 0.2 collective-permute-start.5
  25.6 10.3 %gate_up.5 = (f32[512,2048]{1,0:T(8,128)S(1)}, f32[512,2048]{1,0:T(8,128)S(1)}) custom-call(s32[8]{0:T(128)S(1)} %dynamic-slice_bitcast_fusion.ids_ref, bf16[512,768]{1,0:T(8,128)(2,1)S(1)} %collective-permute-done.refs_0_, bf16[512,768]{1,0:T(8,128)(2,1)S(1)} %collective-permute-done.4.refs_1_, ...), custom_call_target="tpu_custom_call", output_to_operand_aliasing={{0}: (5, {}), {1}: (6, {})} | custom-call | flops 12884901888 | bytes 12582912 | tf_op jit(solution)/shard_map/gate_up/pallas_call | solution.py:176
  35.9 6.4 %collective-permute-done.1.refs_0_ = bf16[512,768]{1,0:T(8,128)(2,1)S(1)} collective-permute-done((bf16[512,768]{1,0:T(8,128)(2,1)S(1)}, bf16[512,768]{1,0:T(8,128)(2,1)S(1)}, u32[]{:S(2)}, u32[]{:S(2)}) %collective-permute-start.1) | collective-permute-done | bytes 786464 | tf_op jit(solution)/shard_map/ppermute | solution.py:303
  42.3 1.5 %collective-permute-start.2 = (bf16[512,768]{1,0:T(8,128)(2,1)S(1)}, bf16[512,768]{1,0:T(8,128)(2,1)S(1)}, u32[]{:S(2)}, u32[]{:S(2)}) collective-permute-start(bf16[512,768]{1,0:T(8,128)(2,1)S(1)} %collective-permute-done.1.refs_0_), channel_id=1, source_target_pairs={{0,2},{2,4},{4,6},{6,7},{7,5},{5,3},{3,1},{1,0},{8,10},{10,12},{12... | collective-permute-start | bytes 2359304 | tf_op jit(solution)/shard_map/ppermute | solution.py:303
  43.9 0.5 collective-permute-start.6
  44.4 10.4 %gate_up.6 = (f32[512,2048]{1,0:T(8,128)S(1)}, f32[512,2048]{1,0:T(8,128)S(1)}, bf16[4,2,768,512]{3,2,1,0:T(8,128)(2,1)S(1)}, bf16[2048,768]{1,0:T(8,128)(2,1)S(1)}) custom-call(s32[8]{0:T(128)S(1)} %dynamic-slice_bitcast_fusion.ids_ref, bf16[512,768]{1,0:T(8,128)(2,1)S(1)} %collective-permute-done.1.refs_0_, ...), custom_call_target="tpu_custom_call", output_to_operand_aliasing={{0}: (6, {}), {1}: (7, {})} | custom-call | flops 12884901888 | bytes 12582912 | tf_op jit(solution)/shard_map/gate_up/pallas_call | solution.py:176
  54.8 5.4 %collective-permute-done.2.refs_0_ = bf16[512,768]{1,0:T(8,128)(2,1)S(1)} collective-permute-done((bf16[512,768]{1,0:T(8,128)(2,1)S(1)}, bf16[512,768]{1,0:T(8,128)(2,1)S(1)}, u32[]{:S(2)}, u32[]{:S(2)}) %collective-permute-start.2) | collective-permute-done | bytes 786464 | tf_op jit(solution)/shard_map/ppermute | solution.py:303
  60.2 1.4 collective-permute-start.3
  61.6 0.0 collective-permute-done.6.refs_1_
  61.6 0.7 collective-permute-start.7
  62.3 10.3 %gate_up.7 = (f32[512,2048]{1,0:T(8,128)S(1)}, f32[512,2048]{1,0:T(8,128)S(1)}) custom-call(s32[8]{0:T(128)S(1)} %dynamic-slice_bitcast_fusion.ids_ref, bf16[512,768]{1,0:T(8,128)(2,1)S(1)} %collective-permute-done.2.refs_0_, bf16[512,768]{1,0:T(8,128)(2,1)S(1)} %collective-permute-done.6.refs_1_, ...), custom_call_target="tpu_custom_call", output_to_operand_aliasing={{0}: (5, {}), {1}: (6, {})} | custom-call | flops 12884901888 | bytes 12582912 | tf_op jit(solution)/shard_map/gate_up/pallas_call | solution.py:176
  72.6 0.0 collective-permute-done.7.bottom_x
  72.6 5.5 %turn.1 = (bf16[512,2048]{1,0:T(8,128)(2,1)S(1)}, bf16[256,768]{1,0:T(8,128)(2,1)S(1)}, bf16[256,768]{1,0:T(8,128)(2,1)S(1)}) custom-call(bf16[256,768]{1,0:T(8,128)(2,1)S(1)} %collective-permute-done.3.top_x, bf16[256,768]{1,0:T(8,128)(2,1)S(1)} %collective-permute-done.7.bottom_x, f32[512,2048]{1,0:T(8,128)S(1)} %get-tuple-element.42.gate_in, ...), custom_call_target="tpu_custom_call" | custom-call | flops 4831838208 | tf_op jit(solution)/shard_map/turn/pallas_call | solution.py:219
  78.2 1.4 collective-permute-start.8
  79.6 0.7 collective-permute-start.9
  80.2 6.9 %down.7 = (f32[512,768]{1,0:T(8,128)S(1)}, f32[512,768]{1,0:T(8,128)S(1)}) custom-call(s32[8]{0:T(128)S(1)} %dynamic-slice_bitcast_fusion.ids_ref, bf16[512,2048]{1,0:T(8,128)(2,1)S(1)} %get-tuple-element.46.hidden_ref, bf16[2048,6144]{1,0:T(8,128)(2,1)} %weight_ref.7), custom_call_target="tpu_custom_call" | custom-call | flops 6442450944 | bytes 6291456 | tf_op jit(solution)/shard_map/down/pallas_call | solution.py:270
  87.2 1.0 collective-permute-done.9
  88.3 0.1 add_convert_fusion.4
  88.3 0.1 pad_maximum_fusion.1
  88.4 0.6 collective-permute-start.11
  89.0 0.1 add_convert_fusion.5
  89.0 0.1 pad_maximum_fusion
  89.1 1.8 %collective-permute-start.10 = (bf16[512,768]{1,0:T(8,128)(2,1)S(1)}, bf16[512,768]{1,0:T(8,128)(2,1)S(1)}, u32[]{:S(2)}, u32[]{:S(2)}) collective-permute-start(bf16[512,768]{1,0:T(8,128)(2,1)S(1)} %pad_maximum_fusion), channel_id=1, source_target_pairs={{0,2},{2,4},{4,6},{6,7},{7,5},{5,3},{3,1},{1,0},{8,10},{10,12},{12... | collective-permute-start | bytes 2359304 | tf_op jit(solution)/shard_map/ppermute | solution.py:303
  90.9 6.9 %down.6 = (f32[512,768]{1,0:T(8,128)S(1)}, f32[512,768]{1,0:T(8,128)S(1)}) custom-call(s32[8]{0:T(128)S(1)} %dynamic-slice_bitcast_fusion.ids_ref, bf16[512,2048]{1,0:T(8,128)(2,1)S(1)} %get-tuple-element.46.hidden_ref, bf16[2048,6144]{1,0:T(8,128)(2,1)} %weight_ref.7), custom_call_target="tpu_custom_call" | custom-call | flops 6442450944 | bytes 6291456 | tf_op jit(solution)/shard_map/down/pallas_call | solution.py:270
  97.8 8.4 %collective-permute-done.11 = bf16[512,768]{1,0:T(8,128)(2,1)S(1)} collective-permute-done((bf16[512,768]{1,0:T(8,128)(2,1)S(1)}, bf16[512,768]{1,0:T(8,128)(2,1)S(1)}, u32[]{:S(2)}, u32[]{:S(2)}) %collective-permute-start.11) | collective-permute-done | bytes 786464 | tf_op jit(solution)/shard_map/ppermute | solution.py:306
  106.2 0.0 collective-permute-done.10
  106.2 0.2 add_convert_fusion.2
  106.4 0.3 collective-permute-start.13
  106.7 0.2 add_convert_fusion.3
  106.9 1.8 %collective-permute-start.12 = (bf16[512,768]{1,0:T(8,128)(2,1)S(1)}, bf16[512,768]{1,0:T(8,128)(2,1)S(1)}, u32[]{:S(2)}, u32[]{:S(2)}) collective-permute-start(bf16[512,768]{1,0:T(8,128)(2,1)S(1)} %add_convert_fusion.3), channel_id=1, source_target_pairs={{0,2},{2,4},{4,6},{6,7},{7,5},{5,3},{3,1},{1,0},{8,10},{10,12},{12... | collective-permute-start | bytes 2359304 | tf_op jit(solution)/shard_map/ppermute | solution.py:303
  108.7 6.8 %down.5 = (f32[512,768]{1,0:T(8,128)S(1)}, f32[512,768]{1,0:T(8,128)S(1)}) custom-call(s32[8]{0:T(128)S(1)} %dynamic-slice_bitcast_fusion.ids_ref, bf16[512,2048]{1,0:T(8,128)(2,1)S(1)} %get-tuple-element.46.hidden_ref, bf16[2048,6144]{1,0:T(8,128)(2,1)} %weight_ref.7), custom_call_target="tpu_custom_call" | custom-call | flops 6442450944 | bytes 6291456 | tf_op jit(solution)/shard_map/down/pallas_call | solution.py:270
  115.5 8.4 %collective-permute-done.13 = bf16[512,768]{1,0:T(8,128)(2,1)S(1)} collective-permute-done((bf16[512,768]{1,0:T(8,128)(2,1)S(1)}, bf16[512,768]{1,0:T(8,128)(2,1)S(1)}, u32[]{:S(2)}, u32[]{:S(2)}) %collective-permute-start.13) | collective-permute-done | bytes 786464 | tf_op jit(solution)/shard_map/ppermute | solution.py:306
  123.9 0.2 add_convert_fusion
  124.1 0.6 collective-permute-start.15
  124.7 0.2 add_convert_fusion.1
  124.8 1.6 %collective-permute-start.14 = (bf16[512,768]{1,0:T(8,128)(2,1)S(1)}, bf16[512,768]{1,0:T(8,128)(2,1)S(1)}, u32[]{:S(2)}, u32[]{:S(2)}) collective-permute-start(bf16[512,768]{1,0:T(8,128)(2,1)S(1)} %add_convert_fusion.1), channel_id=1, source_target_pairs={{0,2},{2,4},{4,6},{6,7},{7,5},{5,3},{3,1},{1,0},{8,10},{10,12},{12... | collective-permute-start | bytes 2359304 | tf_op jit(solution)/shard_map/ppermute | solution.py:303
  126.4 0.3 select_reduce_fusion
  126.7 4.6 %down.4 = f32[512,768]{1,0:T(8,128)S(1)} custom-call(s32[8]{0:T(128)S(1)} %dynamic-slice_bitcast_fusion.ids_ref, bf16[512,2048]{1,0:T(8,128)(2,1)S(1)} %get-tuple-element.46.hidden_ref, bf16[2048,6144]{1,0:T(8,128)(2,1)} %weight_ref.7), custom_call_target="tpu_custom_call" | custom-call | flops 3221225472 | bytes 3145728 | tf_op jit(solution)/shard_map/down/pallas_call | solution.py:270
  131.3 6.6 %collective-permute-done.15 = bf16[512,768]{1,0:T(8,128)(2,1)S(1)} collective-permute-done((bf16[512,768]{1,0:T(8,128)(2,1)S(1)}, bf16[512,768]{1,0:T(8,128)(2,1)S(1)}, u32[]{:S(2)}, u32[]{:S(2)}) %collective-permute-start.15) | collective-permute-done | bytes 786464 | tf_op jit(solution)/shard_map/ppermute | solution.py:306
  137.9 2.5 %fusion.1 = bf16[1024,768]{1,0:T(8,128)(2,1)} fusion(s32[1024]{0:T(1024)S(1)} %bitcast.6, bf16[512,768]{1,0:T(8,128)(2,1)S(1)} %collective-permute-done.15, f32[512,768]{1,0:T(8,128)S(1)} %down.4, bf16[512,768]{1,0:T(8,128)(2,1)S(1)} %collective-permute-done.14, f32[512]{0:T(512)S(1)} %select_reduce_fusion), kind=kOutput, calls=%fused_computation.4 | convolution fusion | flops 808976384 | bytes 4724736 | tf_op jit(solution)/shard_map/dot_general | solution.py:26
  (16 shorter events, 0.2 us)
Async XLA Ops:
  0.0 0.7 copy-start
  3.1 20.5 %collective-permute-start = (bf16[512,768]{1,0:T(8,128)(2,1)S(1)}, bf16[512,768]{1,0:T(8,128)(2,1)S(1)}, u32[]{:S(2)}, u32[]{:S(2)}) collective-permute-start(bf16[512,768]{1,0:T(8,128)(2,1)S(1)} %get-tuple-element.35.refs_0_), channel_id=1, source_target_pairs={{0,2},{2,4},{4,6},{6,7},{7,5},{5,3},{3,1},{1,0},{8,10},{10,12},{12... | collective-permute-start | bytes 2359304 | tf_op jit(solution)/shard_map/ppermute | solution.py:303
  6.2 19.3 %collective-permute-start.4 = (bf16[512,768]{1,0:T(8,128)(2,1)S(1)}, bf16[512,768]{1,0:T(8,128)(2,1)S(1)}, u32[]{:S(2)}, u32[]{:S(2)}) collective-permute-start(bf16[512,768]{1,0:T(8,128)(2,1)S(1)} %get-tuple-element.35.refs_0_), channel_id=1, source_target_pairs={{2,0},{4,2},{6,4},{7,6},{5,7},{3,5},{1,3},{0,1},{10,8},{12,10},{14... | collective-permute-start | bytes 2359304 | tf_op jit(solution)/shard_map/ppermute | solution.py:306
  23.6 18.7 %collective-permute-start.1 = (bf16[512,768]{1,0:T(8,128)(2,1)S(1)}, bf16[512,768]{1,0:T(8,128)(2,1)S(1)}, u32[]{:S(2)}, u32[]{:S(2)}) collective-permute-start(bf16[512,768]{1,0:T(8,128)(2,1)S(1)} %collective-permute-done.refs_0_), channel_id=1, source_target_pairs={{0,2},{2,4},{4,6},{6,7},{7,5},{5,3},{3,1},{1,0},{8,10},{10,12},{12... | collective-permute-start | bytes 2359304 | tf_op jit(solution)/shard_map/ppermute | solution.py:303
  25.4 18.4 %collective-permute-start.5 = (bf16[512,768]{1,0:T(8,128)(2,1)S(1)}, bf16[512,768]{1,0:T(8,128)(2,1)S(1)}, u32[]{:S(2)}, u32[]{:S(2)}) collective-permute-start(bf16[512,768]{1,0:T(8,128)(2,1)S(1)} %collective-permute-done.4.refs_1_), channel_id=1, source_target_pairs={{2,0},{4,2},{6,4},{7,6},{5,7},{3,5},{1,3},{0,1},{10,8},{12,10},{14... | collective-permute-start | bytes 2359304 | tf_op jit(solution)/shard_map/ppermute | solution.py:306
  42.3 17.8 %collective-permute-start.2 = (bf16[512,768]{1,0:T(8,128)(2,1)S(1)}, bf16[512,768]{1,0:T(8,128)(2,1)S(1)}, u32[]{:S(2)}, u32[]{:S(2)}) collective-permute-start(bf16[512,768]{1,0:T(8,128)(2,1)S(1)} %collective-permute-done.1.refs_0_), channel_id=1, source_target_pairs={{0,2},{2,4},{4,6},{6,7},{7,5},{5,3},{3,1},{1,0},{8,10},{10,12},{12... | collective-permute-start | bytes 2359304 | tf_op jit(solution)/shard_map/ppermute | solution.py:303
  43.9 17.7 %collective-permute-start.6 = (bf16[512,768]{1,0:T(8,128)(2,1)S(1)}, bf16[512,768]{1,0:T(8,128)(2,1)S(1)}, u32[]{:S(2)}, u32[]{:S(2)}) collective-permute-start(bf16[512,768]{1,0:T(8,128)(2,1)S(1)} %collective-permute-done.5.refs_1_), channel_id=1, source_target_pairs={{2,0},{4,2},{6,4},{7,6},{5,7},{3,5},{1,3},{0,1},{10,8},{12,10},{14... | collective-permute-start | bytes 2359304 | tf_op jit(solution)/shard_map/ppermute | solution.py:306
  60.2 12.4 %collective-permute-start.3 = (bf16[256,768]{1,0:T(8,128)(2,1)S(1)}, bf16[256,768]{1,0:T(8,128)(2,1)S(1)}, u32[]{:S(2)}, u32[]{:S(2)}) collective-permute-start(bf16[256,768]{1,0:T(8,128)(2,1)S(1)} %slice.26), channel_id=1, source_target_pairs={{0,2},{2,4},{4,6},{6,7},{7,5},{5,3},{3,1},{1,0},{8,10},{10,12},{12... | collective-permute-start | bytes 1179656 | tf_op jit(solution)/shard_map/ppermute | solution.py:303
  61.6 11.0 %collective-permute-start.7 = (bf16[256,768]{1,0:T(8,128)(2,1)S(1)}, bf16[256,768]{1,0:T(8,128)(2,1)S(1)}, u32[]{:S(2)}, u32[]{:S(2)}) collective-permute-start(bf16[256,768]{1,0:T(8,128)(2,1)S(1)} %slice.27), channel_id=1, source_target_pairs={{2,0},{4,2},{6,4},{7,6},{5,7},{3,5},{1,3},{0,1},{10,8},{12,10},{14... | collective-permute-start | bytes 1179656 | tf_op jit(solution)/shard_map/ppermute | solution.py:306
  78.2 9.0 %collective-permute-start.8 = (bf16[256,768]{1,0:T(8,128)(2,1)S(1)}, bf16[256,768]{1,0:T(8,128)(2,1)S(1)}, u32[]{:S(2)}, u32[]{:S(2)}) collective-permute-start(bf16[256,768]{1,0:T(8,128)(2,1)S(1)} %get-tuple-element.50), channel_id=1, source_target_pairs={{0,2},{2,4},{4,6},{6,7},{7,5},{5,3},{3,1},{1,0},{8,10},{10,12},{12... | collective-permute-start | bytes 1179656 | tf_op jit(solution)/shard_map/ppermute | solution.py:303
  79.6 8.7 %collective-permute-start.9 = (bf16[256,768]{1,0:T(8,128)(2,1)S(1)}, bf16[256,768]{1,0:T(8,128)(2,1)S(1)}, u32[]{:S(2)}, u32[]{:S(2)}) collective-permute-start(bf16[256,768]{1,0:T(8,128)(2,1)S(1)} %get-tuple-element.51), channel_id=1, source_target_pairs={{2,0},{4,2},{6,4},{7,6},{5,7},{3,5},{1,3},{0,1},{10,8},{12,10},{14... | collective-permute-start | bytes 1179656 | tf_op jit(solution)/shard_map/ppermute | solution.py:306
  88.4 17.8 %collective-permute-start.11 = (bf16[512,768]{1,0:T(8,128)(2,1)S(1)}, bf16[512,768]{1,0:T(8,128)(2,1)S(1)}, u32[]{:S(2)}, u32[]{:S(2)}) collective-permute-start(bf16[512,768]{1,0:T(8,128)(2,1)S(1)} %pad_maximum_fusion.1), channel_id=1, source_target_pairs={{2,0},{4,2},{6,4},{7,6},{5,7},{3,5},{1,3},{0,1},{10,8},{12,10},{14... | collective-permute-start | bytes 2359304 | tf_op jit(solution)/shard_map/ppermute | solution.py:306
  89.1 17.1 %collective-permute-start.10 = (bf16[512,768]{1,0:T(8,128)(2,1)S(1)}, bf16[512,768]{1,0:T(8,128)(2,1)S(1)}, u32[]{:S(2)}, u32[]{:S(2)}) collective-permute-start(bf16[512,768]{1,0:T(8,128)(2,1)S(1)} %pad_maximum_fusion), channel_id=1, source_target_pairs={{0,2},{2,4},{4,6},{6,7},{7,5},{5,3},{3,1},{1,0},{8,10},{10,12},{12... | collective-permute-start | bytes 2359304 | tf_op jit(solution)/shard_map/ppermute | solution.py:303
  106.4 17.5 %collective-permute-start.13 = (bf16[512,768]{1,0:T(8,128)(2,1)S(1)}, bf16[512,768]{1,0:T(8,128)(2,1)S(1)}, u32[]{:S(2)}, u32[]{:S(2)}) collective-permute-start(bf16[512,768]{1,0:T(8,128)(2,1)S(1)} %add_convert_fusion.2), channel_id=1, source_target_pairs={{2,0},{4,2},{6,4},{7,6},{5,7},{3,5},{1,3},{0,1},{10,8},{12,10},{14... | collective-permute-start | bytes 2359304 | tf_op jit(solution)/shard_map/ppermute | solution.py:306
  106.9 17.0 %collective-permute-start.12 = (bf16[512,768]{1,0:T(8,128)(2,1)S(1)}, bf16[512,768]{1,0:T(8,128)(2,1)S(1)}, u32[]{:S(2)}, u32[]{:S(2)}) collective-permute-start(bf16[512,768]{1,0:T(8,128)(2,1)S(1)} %add_convert_fusion.3), channel_id=1, source_target_pairs={{0,2},{2,4},{4,6},{6,7},{7,5},{5,3},{3,1},{1,0},{8,10},{10,12},{12... | collective-permute-start | bytes 2359304 | tf_op jit(solution)/shard_map/ppermute | solution.py:303
  124.1 13.8 %collective-permute-start.15 = (bf16[512,768]{1,0:T(8,128)(2,1)S(1)}, bf16[512,768]{1,0:T(8,128)(2,1)S(1)}, u32[]{:S(2)}, u32[]{:S(2)}) collective-permute-start(bf16[512,768]{1,0:T(8,128)(2,1)S(1)} %add_convert_fusion), channel_id=1, source_target_pairs={{2,0},{4,2},{6,4},{7,6},{5,7},{3,5},{1,3},{0,1},{10,8},{12,10},{14... | collective-permute-start | bytes 2359304 | tf_op jit(solution)/shard_map/ppermute | solution.py:306
  124.7 1.7 %copy-start.1 = (s32[1024,2]{0,1:T(2,128)S(1)}, s32[1024,2]{0,1:T(2,128)}, u32[]{:S(2)}) copy-start(s32[1024,2]{0,1:T(2,128)} %param.8) | copy-start | bytes 24580
  124.7 1.7 %copy-start.2 = (f32[1024,2]{0,1:T(2,128)S(1)}, f32[1024,2]{0,1:T(2,128)}, u32[]{:S(2)}) copy-start(f32[1024,2]{0,1:T(2,128)} %param.9) | copy-start | bytes 24580
  124.8 13.1 %collective-permute-start.14 = (bf16[512,768]{1,0:T(8,128)(2,1)S(1)}, bf16[512,768]{1,0:T(8,128)(2,1)S(1)}, u32[]{:S(2)}, u32[]{:S(2)}) collective-permute-start(bf16[512,768]{1,0:T(8,128)(2,1)S(1)} %add_convert_fusion.1), channel_id=1, source_target_pairs={{0,2},{2,4},{4,6},{6,7},{7,5},{5,3},{3,1},{1,0},{8,10},{10,12},{12... | collective-permute-start | bytes 2359304 | tf_op jit(solution)/shard_map/ppermute | solution.py:303

commit v3 on v2

--- a/solution.py
+++ b/solution.py
@@ -12,7 +12,6 @@
 TILE = 256
 WIDE = 512
 COST = 2
-AHEAD = 4
 F32 = jnp.float32
 BF16 = jnp.bfloat16
 VMEM_BYTES = 28 * 1024 * 1024
@@ -54,7 +53,13 @@
         select_ref[:, g * LANES : (g + 1) * LANES] = jnp.where(slot_ids == slot, 1.0, 0.0).astype(BF16)
     for k in range(cuts):
         bring(k).wait()
-    chosen_ref[...] = dot(select_ref[...], held_ref[...]).astype(BF16)
+
+    def pick(n, carry):
+        at = pl.ds(pl.multiple_of(n * TILE, TILE), TILE)
+        chosen_ref[:, at] = dot(select_ref[...], held_ref[:, at]).astype(BF16)
+        return carry
+
+    lax.fori_loop(0, held_ref.shape[1] // TILE, pick, 0)
 
 
 def compact(expert_index, tokens, slots):
@@ -70,7 +75,7 @@
         scratch_shapes=[
             pltpu.VMEM((slots, count), BF16),
             pltpu.VMEM((count, width), BF16),
-            pltpu.SemaphoreType.DMA((4,)),
+            pltpu.SemaphoreType.DMA((2,)),
         ],
         compiler_params=params(),
         name="compact",
@@ -81,14 +86,19 @@
     return value / (1.0 + jnp.exp(-value))
 
 
-def gate_up_kernel(ids_ref, *refs, steps, first, fetch):
+def gate_up_kernel(ids_ref, *refs, steps, first, fetch, follow, given):
     xs, refs = refs[: len(steps)], refs[len(steps) :]
     gate_weight, up_weight, *refs = refs
     down_weight, refs = (refs[0], refs[1:]) if fetch is not None else (None, refs)
     gate_in, up_in = (None, None) if first else refs[:2]
     refs = refs if first else refs[2:]
+    given_ref, refs = (refs[0], refs[1:]) if given else (None, refs)
     gate_out, up_out, *refs = refs
-    hold, sem = refs[-2 if fetch is None else -4 :][:2]
+    if fetch is not None:
+        next_ref, down_ref, *refs = refs
+    if follow is not None:
+        follow_ref, *refs = refs
+    hold, sem, *sems = refs
     width = xs[0].shape[1]
     blocks, tile = hold.shape[0], hold.shape[-1]
 
@@ -107,11 +117,7 @@
             for j in range(len(steps)):
                 mine(n, which, j).start()
 
-    def block(n, carry):
-        @pl.when(n + AHEAD < blocks)
-        def _():
-            begin(n + AHEAD)
-
+    def block(n, carry, ready=None):
         @pl.when(n == min(1, blocks - 1))
         def _():
             begin_ahead()
@@ -119,16 +125,17 @@
         at = pl.ds(pl.multiple_of(n * tile, tile), tile)
         x = jnp.concatenate([piece[...] for piece in xs], axis=1)
         for which in range(2):
-            for j in range(len(steps)):
-                mine(n, which, j).wait()
-            value = dot(x, hold[n, which])
+            if ready is None:
+                for j in range(len(steps)):
+                    mine(n, which, j).wait()
+            value = dot(x, hold[n, which] if ready is None else ready[which])
             if not first:
                 value = (gate_in, up_in)[which][:, at] + value
             (gate_out, up_out)[which][:, at] = value
         return carry
 
     if fetch is not None:
-        next_ref, down_ref, _, _, next_sem, down_sem = refs
+        next_sem, down_sem = sems[:2]
         depth, breadth = down_ref.shape
         columns = pl.ds(pl.multiple_of(ids_ref[fetch] * breadth, breadth), breadth)
         below = pltpu.make_async_copy(down_weight.at[:, columns], down_ref, down_sem)
@@ -136,16 +143,30 @@
     def ahead(n, which):
         return copy(n, which, fetch, next_ref.at[n, which], next_sem.at[n, which])
 
+    def after(which, j):
+        width_at = slice(j * width, (j + 1) * width)
+        return copy(0, which, follow[j], follow_ref.at[which, width_at], sems[2].at[which, j])
+
     def begin_ahead():
+        if follow is not None:
+            for which in range(2):
+                for j in range(len(follow)):
+                    after(which, j).start()
         if fetch is not None:
             for n in range(blocks):
                 for which in range(2):
                     ahead(n, which).start()
             below.start()
 
-    for n in range(min(AHEAD, blocks)):
+    for n in range(1 if given else 0, blocks):
         begin(n)
-    lax.fori_loop(0, blocks, block, 0)
+    if given:
+        block(0, 0, given_ref)
+    lax.fori_loop(1 if given else 0, blocks, block, 0)
+    if follow is not None:
+        for which in range(2):
+            for j in range(len(follow)):
+                after(which, j).wait()
     if fetch is not None:
         for n in range(blocks):
             for which in range(2):
@@ -153,7 +174,7 @@
         below.wait()
 
 
-def gate_up(ids, steps, xs, gate_weight, up_weight, sums, down_weight=None, fetch=None):
+def gate_up(ids, steps, xs, gate_weight, up_weight, sums, down_weight=None, fetch=None, follow=None, given=None):
     slots, width = xs[0].shape
     hidden = gate_weight.shape[1]
     first = sums is None
@@ -162,6 +183,7 @@
     weights = [gate_weight, up_weight] + ([] if fetch is None else [down_weight])
     operands = [*xs, *weights, *([] if first else sums)]
     at = 1 + len(operands) - 2
+    operands += [] if given is None else [given]
     blocks = hidden // WIDE
     out_shape = [pltpu.VMEM((slots, hidden), F32)] * 2
     scratch = [
@@ -171,14 +193,20 @@
     if fetch is not None:
         out_shape += [pltpu.VMEM((blocks, 2, width, WIDE), BF16), pltpu.VMEM((hidden, width), BF16)]
         scratch += [pltpu.SemaphoreType.DMA((blocks, 2)), pltpu.SemaphoreType.DMA]
+    if follow is not None:
+        out_shape += [pltpu.VMEM((2, width * len(follow), WIDE), BF16)]
+        scratch += [pltpu.SemaphoreType.DMA((2, len(follow)))]
     flops = 4 * slots * width * hidden * len(steps)
     moved = 4 * width * hidden * len(steps)
     return pl.pallas_call(
-        functools.partial(gate_up_kernel, steps=steps, first=first, fetch=fetch),
+        functools.partial(
+            gate_up_kernel, steps=steps, first=first, fetch=fetch, follow=follow, given=given is not None
+        ),
         in_specs=[pl.BlockSpec(memory_space=pltpu.SMEM)]
         + [on_chip] * len(xs)
         + [away] * len(weights)
-        + [on_chip] * (0 if first else 2),
+        + [on_chip] * (0 if first else 2)
+        + [on_chip] * (0 if given is None else 1),
         out_specs=[on_chip] * len(out_shape),
         out_shape=out_shape,
         scratch_shapes=scratch,
@@ -311,7 +339,7 @@
     own, slot = compact(expert_index, tokens, slots)
 
     right, left = right_of(own), left_of(own)
-    sums = gate_up(ids, [0], [own], gate_weight, up_weight, None)
+    sums, given = gate_up(ids, [0], [own], gate_weight, up_weight, None), None
     for s in range(1, half):
         here = [right, left]
         if s + 1 < half:
@@ -319,11 +347,13 @@
         else:
             right, left = right_of(right[: slots // 2]), left_of(left[slots // 2 :])
         if s == max(1, half - 2):
-            *sums, next_weights, next_down = gate_up(
-                ids, [size - s, s], here, gate_weight, up_weight, sums, down_weight, fetch=half
+            follow = [size - s - 1, s + 1] if s + 1 < half else None
+            gate, up, next_weights, next_down, *more = gate_up(
+                ids, [size - s, s], here, gate_weight, up_weight, sums, down_weight, half, follow
             )
+            sums, given = [gate, up], more[0] if more else None
         else:
-            sums = gate_up(ids, [size - s, s], here, gate_weight, up_weight, sums)
+            sums = gate_up(ids, [size - s, s], here, gate_weight, up_weight, sums, given=given)
     hidden, top, bottom = turn(right, left, sums, next_weights, next_down)
 
     right, left = both(right_of(top), left_of(bottom))

time: 141 us -> 140 us (level)
  transfers between devices with their start and end apart: 16 -> 16, of which waited for: 7 -> 7; matrix products, arithmetic and copies ran while one was open for 1% -> 1% of each run, Pallas kernels for 45% -> 44%
where the time goes in v3:
time: 140 us
  Pallas kernels  70 us (50%)
  waiting for transfers between devices  46.3 us (33%)
  starting transfers between devices  18 us (13%)
  matrix products  2.43 us (2%)
  local copies, waits for them, and re-layouts  1.53 us (1%)
  other arithmetic  1.42 us (1%)
    pallas_call x4, Pallas kernels, gate_up(): pl.pallas_call(functools.partial(gate_up_kernel, steps=steps, first=first...  36.5 us
    pallas_call x4, Pallas kernels, down(): pl.pallas_call(functools.partial(down_kernel, steps=steps), in_specs=[pl....  25.2 us
    ppermute x8, waiting for transfers between devices, left_of(): return lax.ppermute(value, 'tensor', to_left)  24.2 us
    ppermute x8, waiting for transfers between devices, right_of(): return lax.ppermute(value, 'tensor', to_right)  22.1 us
    ppermute x8, starting transfers between devices, right_of(): return lax.ppermute(value, 'tensor', to_right)  14.3 us
    pallas_call x1, Pallas kernels, turn(): pl.pallas_call(turn_kernel, in_specs=[on_chip] * 6, out_specs=[on_chip] *...  5.56 us
    ppermute x8, starting transfers between devices, left_of(): return lax.ppermute(value, 'tensor', to_left)  3.74 us
  transfers between devices with their start and end apart: 16, of which 7 were waited for; matrix products, arithmetic and copies ran while one was open for 1% of the time, Pallas kernels for 44%

profile of v3, /device:TPU:0, one launch (start us, length us, event | category | flops | bytes accessed | tf_op | source)
XLA Modules:
  0.0 139.8 jit_solution(12448488539838850208)
XLA Ops:
  0.0 0.7 copy-done
  0.7 2.7 %compact.1 = (bf16[512,768]{1,0:T(8,128)(2,1)S(1)}, s32[8,128]{1,0:T(8,128)S(1)}) custom-call(s32[2,1024]{1,0:T(2,128)S(1)} %bitcast.4, bf16[1024,768]{1,0:T(8,128)(2,1)} %tokens_ref.1), custom_call_target="tpu_custom_call" | custom-call | tf_op jit(solution)/shard_map/compact/pallas_call | solution.py:68
  3.4 3.1 %collective-permute-start = (bf16[512,768]{1,0:T(8,128)(2,1)S(1)}, bf16[512,768]{1,0:T(8,128)(2,1)S(1)}, u32[]{:S(2)}, u32[]{:S(2)}) collective-permute-start(bf16[512,768]{1,0:T(8,128)(2,1)S(1)} %get-tuple-element.36.refs_0_), channel_id=1, source_target_pairs={{0,2},{2,4},{4,6},{6,7},{7,5},{5,3},{3,1},{1,0},{8,10},{10,12},{12... | collective-permute-start | bytes 2359304 | tf_op jit(solution)/shard_map/ppermute | solution.py:331
  6.5 0.7 dynamic-slice_bitcast_fusion.ids_ref
  7.2 6.5 %gate_up.4 = (f32[512,2048]{1,0:T(8,128)S(1)}, f32[512,2048]{1,0:T(8,128)S(1)}) custom-call(s32[8]{0:T(128)S(1)} %dynamic-slice_bitcast_fusion.ids_ref, bf16[512,768]{1,0:T(8,128)(2,1)S(1)} %get-tuple-element.36.refs_0_, bf16[6144,2048]{1,0:T(8,128)(2,1)} %refs_2_.7, bf16[6144,2048]{1,0:T(8,128)(2,1)} %refs_3_.5), custom_call_target="tpu_custom_call" | custom-call | flops 6442450944 | bytes 6291456 | tf_op jit(solution)/shard_map/gate_up/pallas_call | solution.py:201
  13.7 10.3 %collective-permute-done.refs_0_ = bf16[512,768]{1,0:T(8,128)(2,1)S(1)} collective-permute-done((bf16[512,768]{1,0:T(8,128)(2,1)S(1)}, bf16[512,768]{1,0:T(8,128)(2,1)S(1)}, u32[]{:S(2)}, u32[]{:S(2)}) %collective-permute-start) | collective-permute-done | bytes 786464 | tf_op jit(solution)/shard_map/ppermute | solution.py:331
  24.0 1.8 %collective-permute-start.1 = (bf16[512,768]{1,0:T(8,128)(2,1)S(1)}, bf16[512,768]{1,0:T(8,128)(2,1)S(1)}, u32[]{:S(2)}, u32[]{:S(2)}) collective-permute-start(bf16[512,768]{1,0:T(8,128)(2,1)S(1)} %collective-permute-done.refs_0_), channel_id=1, source_target_pairs={{0,2},{2,4},{4,6},{6,7},{7,5},{5,3},{3,1},{1,0},{8,10},{10,12},{12... | collective-permute-start | bytes 2359304 | tf_op jit(solution)/shard_map/ppermute | solution.py:331
  25.8 0.0 collective-permute-done.4.refs_1_
  25.8 0.2 collective-permute-start.5
  26.0 10.3 %gate_up.5 = (f32[512,2048]{1,0:T(8,128)S(1)}, f32[512,2048]{1,0:T(8,128)S(1)}) custom-call(s32[8]{0:T(128)S(1)} %dynamic-slice_bitcast_fusion.ids_ref, bf16[512,768]{1,0:T(8,128)(2,1)S(1)} %collective-permute-done.refs_0_, bf16[512,768]{1,0:T(8,128)(2,1)S(1)} %collective-permute-done.4.refs_1_, ...), custom_call_target="tpu_custom_call", output_to_operand_aliasing={{0}: (5, {}), {1}: (6, {})} | custom-call | flops 12884901888 | bytes 12582912 | tf_op jit(solution)/shard_map/gate_up/pallas_call | solution.py:201
  36.3 6.4 %collective-permute-done.1.refs_0_ = bf16[512,768]{1,0:T(8,128)(2,1)S(1)} collective-permute-done((bf16[512,768]{1,0:T(8,128)(2,1)S(1)}, bf16[512,768]{1,0:T(8,128)(2,1)S(1)}, u32[]{:S(2)}, u32[]{:S(2)}) %collective-permute-start.1) | collective-permute-done | bytes 786464 | tf_op jit(solution)/shard_map/ppermute | solution.py:331
  42.7 1.5 %collective-permute-start.2 = (bf16[512,768]{1,0:T(8,128)(2,1)S(1)}, bf16[512,768]{1,0:T(8,128)(2,1)S(1)}, u32[]{:S(2)}, u32[]{:S(2)}) collective-permute-start(bf16[512,768]{1,0:T(8,128)(2,1)S(1)} %collective-permute-done.1.refs_0_), channel_id=1, source_target_pairs={{0,2},{2,4},{4,6},{6,7},{7,5},{5,3},{3,1},{1,0},{8,10},{10,12},{12... | collective-permute-start | bytes 2359304 | tf_op jit(solution)/shard_map/ppermute | solution.py:331
  44.2 0.0 collective-permute-done.5.refs_1_
  44.2 0.5 collective-permute-start.6
  44.7 10.4 %gate_up.6 = (f32[512,2048]{1,0:T(8,128)S(1)}, f32[512,2048]{1,0:T(8,128)S(1)}, bf16[4,2,768,512]{3,2,1,0:T(8,128)(2,1)S(1)}, bf16[2048,768]{1,0:T(8,128)(2,1)S(1)}, bf16[2,1536,512]{2,1,0:T(8,128)(2,1)S(1)}) custom-call(s32[8]{0:T(128)S(1)} %dynamic-slice_bitcast_fusion.ids_ref, ...), custom_call_target="tpu_custom_call", output_to_operand_aliasing={{0}: (6, {}), {1}: (7, {})} | custom-call | flops 12884901888 | bytes 12582912 | tf_op jit(solution)/shard_map/gate_up/pallas_call | solution.py:201
  55.1 5.3 %collective-permute-done.2.refs_0_ = bf16[512,768]{1,0:T(8,128)(2,1)S(1)} collective-permute-done((bf16[512,768]{1,0:T(8,128)(2,1)S(1)}, bf16[512,768]{1,0:T(8,128)(2,1)S(1)}, u32[]{:S(2)}, u32[]{:S(2)}) %collective-permute-start.2) | collective-permute-done | bytes 786464 | tf_op jit(solution)/shard_map/ppermute | solution.py:331
  60.5 1.4 collective-permute-start.3
  61.9 0.7 collective-permute-start.7
  62.7 9.4 %gate_up.7 = (f32[512,2048]{1,0:T(8,128)S(1)}, f32[512,2048]{1,0:T(8,128)S(1)}) custom-call(s32[8]{0:T(128)S(1)} %dynamic-slice_bitcast_fusion.ids_ref, bf16[512,768]{1,0:T(8,128)(2,1)S(1)} %collective-permute-done.2.refs_0_, bf16[512,768]{1,0:T(8,128)(2,1)S(1)} %collective-permute-done.6.refs_1_, ...), custom_call_target="tpu_custom_call", output_to_operand_aliasing={{0}: (5, {}), {1}: (6, {})} | custom-call | flops 12884901888 | bytes 12582912 | tf_op jit(solution)/shard_map/gate_up/pallas_call | solution.py:201
  72.1 0.0 collective-permute-done.3.top_x
  72.1 5.6 %turn.1 = (bf16[512,2048]{1,0:T(8,128)(2,1)S(1)}, bf16[256,768]{1,0:T(8,128)(2,1)S(1)}, bf16[256,768]{1,0:T(8,128)(2,1)S(1)}) custom-call(bf16[256,768]{1,0:T(8,128)(2,1)S(1)} %collective-permute-done.3.top_x, bf16[256,768]{1,0:T(8,128)(2,1)S(1)} %collective-permute-done.7.bottom_x, f32[512,2048]{1,0:T(8,128)S(1)} %get-tuple-element.44.gate_in, ...), custom_call_target="tpu_custom_call" | custom-call | flops 4831838208 | tf_op jit(solution)/shard_map/turn/pallas_call | solution.py:247
  77.7 1.4 collective-permute-start.8
  79.0 0.7 collective-permute-start.9
  79.7 6.9 %down.7 = (f32[512,768]{1,0:T(8,128)S(1)}, f32[512,768]{1,0:T(8,128)S(1)}) custom-call(s32[8]{0:T(128)S(1)} %dynamic-slice_bitcast_fusion.ids_ref, bf16[512,2048]{1,0:T(8,128)(2,1)S(1)} %get-tuple-element.48.hidden_ref, bf16[2048,6144]{1,0:T(8,128)(2,1)} %weight_ref.7), custom_call_target="tpu_custom_call" | custom-call | flops 6442450944 | bytes 6291456 | tf_op jit(solution)/shard_map/down/pallas_call | solution.py:298
  86.7 1.0 collective-permute-done.9
  87.7 0.1 add_convert_fusion.4
  87.8 0.1 pad_maximum_fusion.1
  87.9 0.6 collective-permute-start.11
  88.5 0.1 add_convert_fusion.5
  88.6 0.1 pad_maximum_fusion
  88.6 1.8 %collective-permute-start.10 = (bf16[512,768]{1,0:T(8,128)(2,1)S(1)}, bf16[512,768]{1,0:T(8,128)(2,1)S(1)}, u32[]{:S(2)}, u32[]{:S(2)}) collective-permute-start(bf16[512,768]{1,0:T(8,128)(2,1)S(1)} %pad_maximum_fusion), channel_id=1, source_target_pairs={{0,2},{2,4},{4,6},{6,7},{7,5},{5,3},{3,1},{1,0},{8,10},{10,12},{12... | collective-permute-start | bytes 2359304 | tf_op jit(solution)/shard_map/ppermute | solution.py:331
  90.4 6.9 %down.6 = (f32[512,768]{1,0:T(8,128)S(1)}, f32[512,768]{1,0:T(8,128)S(1)}) custom-call(s32[8]{0:T(128)S(1)} %dynamic-slice_bitcast_fusion.ids_ref, bf16[512,2048]{1,0:T(8,128)(2,1)S(1)} %get-tuple-element.48.hidden_ref, bf16[2048,6144]{1,0:T(8,128)(2,1)} %weight_ref.7), custom_call_target="tpu_custom_call" | custom-call | flops 6442450944 | bytes 6291456 | tf_op jit(solution)/shard_map/down/pallas_call | solution.py:298
  97.3 8.4 %collective-permute-done.11 = bf16[512,768]{1,0:T(8,128)(2,1)S(1)} collective-permute-done((bf16[512,768]{1,0:T(8,128)(2,1)S(1)}, bf16[512,768]{1,0:T(8,128)(2,1)S(1)}, u32[]{:S(2)}, u32[]{:S(2)}) %collective-permute-start.11) | collective-permute-done | bytes 786464 | tf_op jit(solution)/shard_map/ppermute | solution.py:334
  105.6 0.0 collective-permute-done.10
  105.6 0.2 add_convert_fusion.2
  105.8 0.3 collective-permute-start.13
  106.2 0.2 add_convert_fusion.3
  106.4 1.8 %collective-permute-start.12 = (bf16[512,768]{1,0:T(8,128)(2,1)S(1)}, bf16[512,768]{1,0:T(8,128)(2,1)S(1)}, u32[]{:S(2)}, u32[]{:S(2)}) collective-permute-start(bf16[512,768]{1,0:T(8,128)(2,1)S(1)} %add_convert_fusion.3), channel_id=1, source_target_pairs={{0,2},{2,4},{4,6},{6,7},{7,5},{5,3},{3,1},{1,0},{8,10},{10,12},{12... | collective-permute-start | bytes 2359304 | tf_op jit(solution)/shard_map/ppermute | solution.py:331
  108.2 6.9 %down.5 = (f32[512,768]{1,0:T(8,128)S(1)}, f32[512,768]{1,0:T(8,128)S(1)}) custom-call(s32[8]{0:T(128)S(1)} %dynamic-slice_bitcast_fusion.ids_ref, bf16[512,2048]{1,0:T(8,128)(2,1)S(1)} %get-tuple-element.48.hidden_ref, bf16[2048,6144]{1,0:T(8,128)(2,1)} %weight_ref.7), custom_call_target="tpu_custom_call" | custom-call | flops 6442450944 | bytes 6291456 | tf_op jit(solution)/shard_map/down/pallas_call | solution.py:298
  115.0 8.3 %collective-permute-done.13 = bf16[512,768]{1,0:T(8,128)(2,1)S(1)} collective-permute-done((bf16[512,768]{1,0:T(8,128)(2,1)S(1)}, bf16[512,768]{1,0:T(8,128)(2,1)S(1)}, u32[]{:S(2)}, u32[]{:S(2)}) %collective-permute-start.13) | collective-permute-done | bytes 786464 | tf_op jit(solution)/shard_map/ppermute | solution.py:334
  123.3 0.2 add_convert_fusion
  123.5 0.6 collective-permute-start.15
  124.2 0.2 add_convert_fusion.1
  124.4 1.5 %collective-permute-start.14 = (bf16[512,768]{1,0:T(8,128)(2,1)S(1)}, bf16[512,768]{1,0:T(8,128)(2,1)S(1)}, u32[]{:S(2)}, u32[]{:S(2)}) collective-permute-start(bf16[512,768]{1,0:T(8,128)(2,1)S(1)} %add_convert_fusion.1), channel_id=1, source_target_pairs={{0,2},{2,4},{4,6},{6,7},{7,5},{5,3},{3,1},{1,0},{8,10},{10,12},{12... | collective-permute-start | bytes 2359304 | tf_op jit(solution)/shard_map/ppermute | solution.py:331
  125.9 0.3 select_reduce_fusion
  126.2 4.6 %down.4 = f32[512,768]{1,0:T(8,128)S(1)} custom-call(s32[8]{0:T(128)S(1)} %dynamic-slice_bitcast_fusion.ids_ref, bf16[512,2048]{1,0:T(8,128)(2,1)S(1)} %get-tuple-element.48.hidden_ref, bf16[2048,6144]{1,0:T(8,128)(2,1)} %weight_ref.7), custom_call_target="tpu_custom_call" | custom-call | flops 3221225472 | bytes 3145728 | tf_op jit(solution)/shard_map/down/pallas_call | solution.py:298
  130.8 6.5 %collective-permute-done.15 = bf16[512,768]{1,0:T(8,128)(2,1)S(1)} collective-permute-done((bf16[512,768]{1,0:T(8,128)(2,1)S(1)}, bf16[512,768]{1,0:T(8,128)(2,1)S(1)}, u32[]{:S(2)}, u32[]{:S(2)}) %collective-permute-start.15) | collective-permute-done | bytes 786464 | tf_op jit(solution)/shard_map/ppermute | solution.py:334
  137.4 2.4 %fusion.1 = bf16[1024,768]{1,0:T(8,128)(2,1)} fusion(s32[1024]{0:T(1024)S(1)} %bitcast.6, bf16[512,768]{1,0:T(8,128)(2,1)S(1)} %collective-permute-done.15, f32[512,768]{1,0:T(8,128)S(1)} %down.4, bf16[512,768]{1,0:T(8,128)(2,1)S(1)} %collective-permute-done.14, f32[512]{0:T(512)S(1)} %select_reduce_fusion), kind=kOutput, calls=%fused_computation.4 | convolution fusion | flops 808976384 | bytes 4724736 | tf_op jit(solution)/shard_map/dot_general | solution.py:25
  (16 shorter events, 0.2 us)
Async XLA Ops:
  0.0 0.7 copy-start
  3.4 20.5 %collective-permute-start = (bf16[512,768]{1,0:T(8,128)(2,1)S(1)}, bf16[512,768]{1,0:T(8,128)(2,1)S(1)}, u32[]{:S(2)}, u32[]{:S(2)}) collective-permute-start(bf16[512,768]{1,0:T(8,128)(2,1)S(1)} %get-tuple-element.36.refs_0_), channel_id=1, source_target_pairs={{0,2},{2,4},{4,6},{6,7},{7,5},{5,3},{3,1},{1,0},{8,10},{10,12},{12... | collective-permute-start | bytes 2359304 | tf_op jit(solution)/shard_map/ppermute | solution.py:331
  6.5 19.3 %collective-permute-start.4 = (bf16[512,768]{1,0:T(8,128)(2,1)S(1)}, bf16[512,768]{1,0:T(8,128)(2,1)S(1)}, u32[]{:S(2)}, u32[]{:S(2)}) collective-permute-start(bf16[512,768]{1,0:T(8,128)(2,1)S(1)} %get-tuple-element.36.refs_0_), channel_id=1, source_target_pairs={{2,0},{4,2},{6,4},{7,6},{5,7},{3,5},{1,3},{0,1},{10,8},{12,10},{14... | collective-permute-start | bytes 2359304 | tf_op jit(solution)/shard_map/ppermute | solution.py:334
  24.0 18.7 %collective-permute-start.1 = (bf16[512,768]{1,0:T(8,128)(2,1)S(1)}, bf16[512,768]{1,0:T(8,128)(2,1)S(1)}, u32[]{:S(2)}, u32[]{:S(2)}) collective-permute-start(bf16[512,768]{1,0:T(8,128)(2,1)S(1)} %collective-permute-done.refs_0_), channel_id=1, source_target_pairs={{0,2},{2,4},{4,6},{6,7},{7,5},{5,3},{3,1},{1,0},{8,10},{10,12},{12... | collective-permute-start | bytes 2359304 | tf_op jit(solution)/shard_map/ppermute | solution.py:331
  25.8 18.4 %collective-permute-start.5 = (bf16[512,768]{1,0:T(8,128)(2,1)S(1)}, bf16[512,768]{1,0:T(8,128)(2,1)S(1)}, u32[]{:S(2)}, u32[]{:S(2)}) collective-permute-start(bf16[512,768]{1,0:T(8,128)(2,1)S(1)} %collective-permute-done.4.refs_1_), channel_id=1, source_target_pairs={{2,0},{4,2},{6,4},{7,6},{5,7},{3,5},{1,3},{0,1},{10,8},{12,10},{14... | collective-permute-start | bytes 2359304 | tf_op jit(solution)/shard_map/ppermute | solution.py:334
  42.7 17.8 %collective-permute-start.2 = (bf16[512,768]{1,0:T(8,128)(2,1)S(1)}, bf16[512,768]{1,0:T(8,128)(2,1)S(1)}, u32[]{:S(2)}, u32[]{:S(2)}) collective-permute-start(bf16[512,768]{1,0:T(8,128)(2,1)S(1)} %collective-permute-done.1.refs_0_), channel_id=1, source_target_pairs={{0,2},{2,4},{4,6},{6,7},{7,5},{5,3},{3,1},{1,0},{8,10},{10,12},{12... | collective-permute-start | bytes 2359304 | tf_op jit(solution)/shard_map/ppermute | solution.py:331
  44.2 17.7 %collective-permute-start.6 = (bf16[512,768]{1,0:T(8,128)(2,1)S(1)}, bf16[512,768]{1,0:T(8,128)(2,1)S(1)}, u32[]{:S(2)}, u32[]{:S(2)}) collective-permute-start(bf16[512,768]{1,0:T(8,128)(2,1)S(1)} %collective-permute-done.5.refs_1_), channel_id=1, source_target_pairs={{2,0},{4,2},{6,4},{7,6},{5,7},{3,5},{1,3},{0,1},{10,8},{12,10},{14... | collective-permute-start | bytes 2359304 | tf_op jit(solution)/shard_map/ppermute | solution.py:334
  60.5 11.6 %collective-permute-start.3 = (bf16[256,768]{1,0:T(8,128)(2,1)S(1)}, bf16[256,768]{1,0:T(8,128)(2,1)S(1)}, u32[]{:S(2)}, u32[]{:S(2)}) collective-permute-start(bf16[256,768]{1,0:T(8,128)(2,1)S(1)} %slice.26), channel_id=1, source_target_pairs={{0,2},{2,4},{4,6},{6,7},{7,5},{5,3},{3,1},{1,0},{8,10},{10,12},{12... | collective-permute-start | bytes 1179656 | tf_op jit(solution)/shard_map/ppermute | solution.py:331
  61.9 10.2 %collective-permute-start.7 = (bf16[256,768]{1,0:T(8,128)(2,1)S(1)}, bf16[256,768]{1,0:T(8,128)(2,1)S(1)}, u32[]{:S(2)}, u32[]{:S(2)}) collective-permute-start(bf16[256,768]{1,0:T(8,128)(2,1)S(1)} %slice.27), channel_id=1, source_target_pairs={{2,0},{4,2},{6,4},{7,6},{5,7},{3,5},{1,3},{0,1},{10,8},{12,10},{14... | collective-permute-start | bytes 1179656 | tf_op jit(solution)/shard_map/ppermute | solution.py:334
  77.7 9.0 %collective-permute-start.8 = (bf16[256,768]{1,0:T(8,128)(2,1)S(1)}, bf16[256,768]{1,0:T(8,128)(2,1)S(1)}, u32[]{:S(2)}, u32[]{:S(2)}) collective-permute-start(bf16[256,768]{1,0:T(8,128)(2,1)S(1)} %get-tuple-element.52), channel_id=1, source_target_pairs={{0,2},{2,4},{4,6},{6,7},{7,5},{5,3},{3,1},{1,0},{8,10},{10,12},{12... | collective-permute-start | bytes 1179656 | tf_op jit(solution)/shard_map/ppermute | solution.py:331
  79.0 8.7 %collective-permute-start.9 = (bf16[256,768]{1,0:T(8,128)(2,1)S(1)}, bf16[256,768]{1,0:T(8,128)(2,1)S(1)}, u32[]{:S(2)}, u32[]{:S(2)}) collective-permute-start(bf16[256,768]{1,0:T(8,128)(2,1)S(1)} %get-tuple-element.53), channel_id=1, source_target_pairs={{2,0},{4,2},{6,4},{7,6},{5,7},{3,5},{1,3},{0,1},{10,8},{12,10},{14... | collective-permute-start | bytes 1179656 | tf_op jit(solution)/shard_map/ppermute | solution.py:334
  87.9 17.8 %collective-permute-start.11 = (bf16[512,768]{1,0:T(8,128)(2,1)S(1)}, bf16[512,768]{1,0:T(8,128)(2,1)S(1)}, u32[]{:S(2)}, u32[]{:S(2)}) collective-permute-start(bf16[512,768]{1,0:T(8,128)(2,1)S(1)} %pad_maximum_fusion.1), channel_id=1, source_target_pairs={{2,0},{4,2},{6,4},{7,6},{5,7},{3,5},{1,3},{0,1},{10,8},{12,10},{14... | collective-permute-start | bytes 2359304 | tf_op jit(solution)/shard_map/ppermute | solution.py:334
  88.6 17.0 %collective-permute-start.10 = (bf16[512,768]{1,0:T(8,128)(2,1)S(1)}, bf16[512,768]{1,0:T(8,128)(2,1)S(1)}, u32[]{:S(2)}, u32[]{:S(2)}) collective-permute-start(bf16[512,768]{1,0:T(8,128)(2,1)S(1)} %pad_maximum_fusion), channel_id=1, source_target_pairs={{0,2},{2,4},{4,6},{6,7},{7,5},{5,3},{3,1},{1,0},{8,10},{10,12},{12... | collective-permute-start | bytes 2359304 | tf_op jit(solution)/shard_map/ppermute | solution.py:331
  105.8 17.5 %collective-permute-start.13 = (bf16[512,768]{1,0:T(8,128)(2,1)S(1)}, bf16[512,768]{1,0:T(8,128)(2,1)S(1)}, u32[]{:S(2)}, u32[]{:S(2)}) collective-permute-start(bf16[512,768]{1,0:T(8,128)(2,1)S(1)} %add_convert_fusion.2), channel_id=1, source_target_pairs={{2,0},{4,2},{6,4},{7,6},{5,7},{3,5},{1,3},{0,1},{10,8},{12,10},{14... | collective-permute-start | bytes 2359304 | tf_op jit(solution)/shard_map/ppermute | solution.py:334
  106.4 16.9 %collective-permute-start.12 = (bf16[512,768]{1,0:T(8,128)(2,1)S(1)}, bf16[512,768]{1,0:T(8,128)(2,1)S(1)}, u32[]{:S(2)}, u32[]{:S(2)}) collective-permute-start(bf16[512,768]{1,0:T(8,128)(2,1)S(1)} %add_convert_fusion.3), channel_id=1, source_target_pairs={{0,2},{2,4},{4,6},{6,7},{7,5},{5,3},{3,1},{1,0},{8,10},{10,12},{12... | collective-permute-start | bytes 2359304 | tf_op jit(solution)/shard_map/ppermute | solution.py:331
  123.5 13.8 %collective-permute-start.15 = (bf16[512,768]{1,0:T(8,128)(2,1)S(1)}, bf16[512,768]{1,0:T(8,128)(2,1)S(1)}, u32[]{:S(2)}, u32[]{:S(2)}) collective-permute-start(bf16[512,768]{1,0:T(8,128)(2,1)S(1)} %add_convert_fusion), channel_id=1, source_target_pairs={{2,0},{4,2},{6,4},{7,6},{5,7},{3,5},{1,3},{0,1},{10,8},{12,10},{14... | collective-permute-start | bytes 2359304 | tf_op jit(solution)/shard_map/ppermute | solution.py:334
  124.2 1.7 %copy-start.1 = (s32[1024,2]{0,1:T(2,128)S(1)}, s32[1024,2]{0,1:T(2,128)}, u32[]{:S(2)}) copy-start(s32[1024,2]{0,1:T(2,128)} %param.8) | copy-start | bytes 24580
  124.2 1.7 %copy-start.2 = (f32[1024,2]{0,1:T(2,128)S(1)}, f32[1024,2]{0,1:T(2,128)}, u32[]{:S(2)}) copy-start(f32[1024,2]{0,1:T(2,128)} %param.9) | copy-start | bytes 24580
  124.4 13.0 %collective-permute-start.14 = (bf16[512,768]{1,0:T(8,128)(2,1)S(1)}, bf16[512,768]{1,0:T(8,128)(2,1)S(1)}, u32[]{:S(2)}, u32[]{:S(2)}) collective-permute-start(bf16[512,768]{1,0:T(8,128)(2,1)S(1)} %add_convert_fusion.1), channel_id=1, source_target_pairs={{0,2},{2,4},{4,6},{6,7},{7,5},{5,3},{3,1},{1,0},{8,10},{10,12},{12... | collective-permute-start | bytes 2359304 | tf_op jit(solution)/shard_map/ppermute | solution.py:331

commit v4 on v3

--- a/solution.py
+++ b/solution.py
@@ -261,35 +261,34 @@
     )(top, bottom, *sums, next_weights, next_down)
 
 
-def down_kernel(ids_ref, hidden_ref, weight_ref, *refs, steps):
-    outs, hold, sem = refs[:-2], *refs[-2:]
+def down_kernel(ids_ref, hidden_ref, weight_ref, out_ref, hold, sem, *, steps):
     width = hold.shape[-1]
     depth = hidden_ref.shape[1]
     cuts = sem.shape[1]
     deep = depth // cuts
-
-    def copy(i, k):
-        columns = pl.ds(pl.multiple_of(ids_ref[steps[i]] * width, width), width)
+    tiles = width // TILE
+
+    def copy(i, k, step):
+        columns = pl.ds(pl.multiple_of(ids_ref[step] * width, width), width)
         rows = slice(k * deep, (k + 1) * deep)
         return pltpu.make_async_copy(weight_ref.at[rows, columns], hold.at[i, rows], sem.at[i, k])
 
-    for k in range(cuts):
-        copy(0, k).start()
-    for i in range(len(steps)):
-
-        def block(n, carry, i=i):
-            @pl.when(n == 0)
-            def _():
-                for k in range(cuts):
-                    copy(i, k).wait()
-                    if i + 1 < len(steps):
-                        copy(i + 1, k).start()
-
-            at = pl.ds(pl.multiple_of(n * TILE, TILE), TILE)
-            outs[i][:, at] = dot(hidden_ref[...], hold[i, :, at])
-            return carry
-
-        lax.fori_loop(0, width // TILE, block, 0)
+    def block(t, carry):
+        i, n = t // tiles, t % tiles
+
+        @pl.when(n == 0)
+        def _():
+            for k in range(cuts):
+                copy(i, k, steps[0]).wait()
+
+        at = pl.ds(pl.multiple_of(n * TILE, TILE), TILE)
+        out_ref[i, :, at] = dot(hidden_ref[...], hold[i, :, at])
+        return carry
+
+    for i, step in enumerate(steps):
+        for k in range(cuts):
+            copy(i, k, step).start()
+    lax.fori_loop(0, len(steps) * tiles, block, 0)
 
 
 def down(ids, steps, hidden, down_weight, width):
@@ -298,8 +297,8 @@
     return pl.pallas_call(
         functools.partial(down_kernel, steps=steps),
         in_specs=[pl.BlockSpec(memory_space=pltpu.SMEM), on_chip, pl.BlockSpec(memory_space=pl.ANY)],
-        out_specs=(on_chip,) * len(steps),
-        out_shape=(jax.ShapeDtypeStruct((slots, width), F32),) * len(steps),
+        out_specs=on_chip,
+        out_shape=jax.ShapeDtypeStruct((len(steps), slots, width), F32),
         scratch_shapes=[
             pltpu.VMEM((len(steps), depth, width), BF16),
             pltpu.SemaphoreType.DMA((len(steps), 4)),

time: 140 us -> 140 us (level)
    ppermute x8, waiting for transfers between devices: 24.2 us -> 8.06 us  [left_of(): return lax.ppermute(value, 'tensor', to_left)]
    ppermute x8, waiting for transfers between devices: 22.1 us -> 37.9 us  [right_of(): return lax.ppermute(value, 'tensor', to_right)]
  transfers between devices with their start and end apart: 16 -> 16, of which waited for: 7 -> 9; matrix products, arithmetic and copies ran while one was open for 1% -> 1% of each run, Pallas kernels for 44% -> 44%
where the time goes in v4:
time: 140 us
  Pallas kernels  70 us (50%)
  waiting for transfers between devices  46 us (33%)
  starting transfers between devices  18 us (13%)
  matrix products  2.43 us (2%)
  other arithmetic  1.69 us (1%)
  local copies, waits for them, and re-layouts  1.51 us (1%)
    ppermute x8, waiting for transfers between devices, right_of(): return lax.ppermute(value, 'tensor', to_right)  37.9 us
    pallas_call x4, Pallas kernels, gate_up(): pl.pallas_call(functools.partial(gate_up_kernel, steps=steps, first=first...  36.5 us
    pallas_call x4, Pallas kernels, down(): pl.pallas_call(functools.partial(down_kernel, steps=steps), in_specs=[pl....  25.2 us
    ppermute x8, starting transfers between devices, right_of(): return lax.ppermute(value, 'tensor', to_right)  13.4 us
    ppermute x8, waiting for transfers between devices, left_of(): return lax.ppermute(value, 'tensor', to_left)  8.06 us
    pallas_call x1, Pallas kernels, turn(): pl.pallas_call(turn_kernel, in_specs=[on_chip] * 6, out_specs=[on_chip] *...  5.56 us
    ppermute x8, starting transfers between devices, left_of(): return lax.ppermute(value, 'tensor', to_left)  4.65 us
  transfers between devices with their start and end apart: 16, of which 9 were waited for; matrix products, arithmetic and copies ran while one was open for 1% of the time, Pallas kernels for 44%

profile of v4, /device:TPU:0, one launch (start us, length us, event | category | flops | bytes accessed | tf_op | source)
XLA Modules:
  0.0 139.8 jit_solution(3438038107599932379)
XLA Ops:
  0.0 0.7 copy-done
  0.7 2.7 %compact.1 = (bf16[512,768]{1,0:T(8,128)(2,1)S(1)}, s32[8,128]{1,0:T(8,128)S(1)}) custom-call(s32[2,1024]{1,0:T(2,128)S(1)} %bitcast.53, bf16[1024,768]{1,0:T(8,128)(2,1)} %tokens_ref.1), custom_call_target="tpu_custom_call" | custom-call | tf_op jit(solution)/shard_map/compact/pallas_call | solution.py:68
  3.4 3.1 %collective-permute-start = (bf16[512,768]{1,0:T(8,128)(2,1)S(1)}, bf16[512,768]{1,0:T(8,128)(2,1)S(1)}, u32[]{:S(2)}, u32[]{:S(2)}) collective-permute-start(bf16[512,768]{1,0:T(8,128)(2,1)S(1)} %get-tuple-element.30.refs_0_), channel_id=1, source_target_pairs={{0,2},{2,4},{4,6},{6,7},{7,5},{5,3},{3,1},{1,0},{8,10},{10,12},{12... | collective-permute-start | bytes 2359304 | tf_op jit(solution)/shard_map/ppermute | solution.py:330
  6.5 0.7 dynamic-slice_bitcast_fusion.ids_ref
  7.2 6.5 %gate_up.4 = (f32[512,2048]{1,0:T(8,128)S(1)}, f32[512,2048]{1,0:T(8,128)S(1)}) custom-call(s32[8]{0:T(128)S(1)} %dynamic-slice_bitcast_fusion.ids_ref, bf16[512,768]{1,0:T(8,128)(2,1)S(1)} %get-tuple-element.30.refs_0_, bf16[6144,2048]{1,0:T(8,128)(2,1)} %refs_2_.7, bf16[6144,2048]{1,0:T(8,128)(2,1)} %refs_3_.5), custom_call_target="tpu_custom_call" | custom-call | flops 6442450944 | bytes 6291456 | tf_op jit(solution)/shard_map/gate_up/pallas_call | solution.py:201
  13.7 10.3 %collective-permute-done.refs_0_ = bf16[512,768]{1,0:T(8,128)(2,1)S(1)} collective-permute-done((bf16[512,768]{1,0:T(8,128)(2,1)S(1)}, bf16[512,768]{1,0:T(8,128)(2,1)S(1)}, u32[]{:S(2)}, u32[]{:S(2)}) %collective-permute-start) | collective-permute-done | bytes 786464 | tf_op jit(solution)/shard_map/ppermute | solution.py:330
  24.0 1.8 %collective-permute-start.1 = (bf16[512,768]{1,0:T(8,128)(2,1)S(1)}, bf16[512,768]{1,0:T(8,128)(2,1)S(1)}, u32[]{:S(2)}, u32[]{:S(2)}) collective-permute-start(bf16[512,768]{1,0:T(8,128)(2,1)S(1)} %collective-permute-done.refs_0_), channel_id=1, source_target_pairs={{0,2},{2,4},{4,6},{6,7},{7,5},{5,3},{3,1},{1,0},{8,10},{10,12},{12... | collective-permute-start | bytes 2359304 | tf_op jit(solution)/shard_map/ppermute | solution.py:330
  25.8 0.0 collective-permute-done.4.refs_1_
  25.8 0.2 collective-permute-start.5
  26.0 10.3 %gate_up.5 = (f32[512,2048]{1,0:T(8,128)S(1)}, f32[512,2048]{1,0:T(8,128)S(1)}) custom-call(s32[8]{0:T(128)S(1)} %dynamic-slice_bitcast_fusion.ids_ref, bf16[512,768]{1,0:T(8,128)(2,1)S(1)} %collective-permute-done.refs_0_, bf16[512,768]{1,0:T(8,128)(2,1)S(1)} %collective-permute-done.4.refs_1_, ...), custom_call_target="tpu_custom_call", output_to_operand_aliasing={{0}: (5, {}), {1}: (6, {})} | custom-call | flops 12884901888 | bytes 12582912 | tf_op jit(solution)/shard_map/gate_up/pallas_call | solution.py:201
  36.3 6.4 %collective-permute-done.1.refs_0_ = bf16[512,768]{1,0:T(8,128)(2,1)S(1)} collective-permute-done((bf16[512,768]{1,0:T(8,128)(2,1)S(1)}, bf16[512,768]{1,0:T(8,128)(2,1)S(1)}, u32[]{:S(2)}, u32[]{:S(2)}) %collective-permute-start.1) | collective-permute-done | bytes 786464 | tf_op jit(solution)/shard_map/ppermute | solution.py:330
  42.7 1.5 %collective-permute-start.2 = (bf16[512,768]{1,0:T(8,128)(2,1)S(1)}, bf16[512,768]{1,0:T(8,128)(2,1)S(1)}, u32[]{:S(2)}, u32[]{:S(2)}) collective-permute-start(bf16[512,768]{1,0:T(8,128)(2,1)S(1)} %collective-permute-done.1.refs_0_), channel_id=1, source_target_pairs={{0,2},{2,4},{4,6},{6,7},{7,5},{5,3},{3,1},{1,0},{8,10},{10,12},{12... | collective-permute-start | bytes 2359304 | tf_op jit(solution)/shard_map/ppermute | solution.py:330
  44.2 0.5 collective-permute-start.6
  44.7 10.4 %gate_up.6 = (f32[512,2048]{1,0:T(8,128)S(1)}, f32[512,2048]{1,0:T(8,128)S(1)}, bf16[4,2,768,512]{3,2,1,0:T(8,128)(2,1)S(1)}, bf16[2048,768]{1,0:T(8,128)(2,1)S(1)}, bf16[2,1536,512]{2,1,0:T(8,128)(2,1)S(1)}) custom-call(s32[8]{0:T(128)S(1)} %dynamic-slice_bitcast_fusion.ids_ref, ...), custom_call_target="tpu_custom_call", output_to_operand_aliasing={{0}: (6, {}), {1}: (7, {})} | custom-call | flops 12884901888 | bytes 12582912 | tf_op jit(solution)/shard_map/gate_up/pallas_call | solution.py:201
  55.1 5.3 %collective-permute-done.2.refs_0_ = bf16[512,768]{1,0:T(8,128)(2,1)S(1)} collective-permute-done((bf16[512,768]{1,0:T(8,128)(2,1)S(1)}, bf16[512,768]{1,0:T(8,128)(2,1)S(1)}, u32[]{:S(2)}, u32[]{:S(2)}) %collective-permute-start.2) | collective-permute-done | bytes 786464 | tf_op jit(solution)/shard_map/ppermute | solution.py:330
  60.5 1.4 collective-permute-start.3
  61.9 0.7 collective-permute-start.7
  62.7 9.4 %gate_up.7 = (f32[512,2048]{1,0:T(8,128)S(1)}, f32[512,2048]{1,0:T(8,128)S(1)}) custom-call(s32[8]{0:T(128)S(1)} %dynamic-slice_bitcast_fusion.ids_ref, bf16[512,768]{1,0:T(8,128)(2,1)S(1)} %collective-permute-done.2.refs_0_, bf16[512,768]{1,0:T(8,128)(2,1)S(1)} %collective-permute-done.6.refs_1_, ...), custom_call_target="tpu_custom_call", output_to_operand_aliasing={{0}: (5, {}), {1}: (6, {})} | custom-call | flops 12884901888 | bytes 12582912 | tf_op jit(solution)/shard_map/gate_up/pallas_call | solution.py:201
  72.1 5.6 %turn.1 = (bf16[512,2048]{1,0:T(8,128)(2,1)S(1)}, bf16[256,768]{1,0:T(8,128)(2,1)S(1)}, bf16[256,768]{1,0:T(8,128)(2,1)S(1)}) custom-call(bf16[256,768]{1,0:T(8,128)(2,1)S(1)} %collective-permute-done.3.top_x, bf16[256,768]{1,0:T(8,128)(2,1)S(1)} %collective-permute-done.7.bottom_x, f32[512,2048]{1,0:T(8,128)S(1)} %get-tuple-element.38.gate_in, ...), custom_call_target="tpu_custom_call" | custom-call | flops 4831838208 | tf_op jit(solution)/shard_map/turn/pallas_call | solution.py:247
  77.7 1.4 collective-permute-start.8
  79.0 0.7 collective-permute-start.9
  79.7 6.9 %down.7 = f32[2,512,768]{2,1,0:T(8,128)S(1)} custom-call(s32[8]{0:T(128)S(1)} %dynamic-slice_bitcast_fusion.ids_ref, bf16[512,2048]{1,0:T(8,128)(2,1)S(1)} %get-tuple-element.42.hidden_ref, bf16[2048,6144]{1,0:T(8,128)(2,1)} %weight_ref.7), custom_call_target="tpu_custom_call" | custom-call | flops 6442450944 | bytes 6291456 | tf_op jit(solution)/shard_map/down/pallas_call | solution.py:297
  86.6 0.2 convert.15
  86.8 0.1 slice_bitcast_fusion.6
  86.8 0.7 collective-permute-done.9
  87.5 0.2 fusion.16
  87.7 0.1 pad_maximum_fusion.1
  87.7 0.6 collective-permute-start.11
  88.4 0.1 pad_maximum_fusion
  88.4 1.7 %collective-permute-start.10 = (bf16[512,768]{1,0:T(8,128)(2,1)S(1)}, bf16[512,768]{1,0:T(8,128)(2,1)S(1)}, u32[]{:S(2)}, u32[]{:S(2)}) collective-permute-start(bf16[512,768]{1,0:T(8,128)(2,1)S(1)} %pad_maximum_fusion), channel_id=1, source_target_pairs={{0,2},{2,4},{4,6},{6,7},{7,5},{5,3},{3,1},{1,0},{8,10},{10,12},{12... | collective-permute-start | bytes 2359304 | tf_op jit(solution)/shard_map/ppermute | solution.py:330
  90.2 6.9 %down.6 = f32[2,512,768]{2,1,0:T(8,128)S(1)} custom-call(s32[8]{0:T(128)S(1)} %dynamic-slice_bitcast_fusion.ids_ref, bf16[512,2048]{1,0:T(8,128)(2,1)S(1)} %get-tuple-element.42.hidden_ref, bf16[2048,6144]{1,0:T(8,128)(2,1)} %weight_ref.7), custom_call_target="tpu_custom_call" | custom-call | flops 6442450944 | bytes 6291456 | tf_op jit(solution)/shard_map/down/pallas_call | solution.py:297
  97.0 7.3 %collective-permute-done.11 = bf16[512,768]{1,0:T(8,128)(2,1)S(1)} collective-permute-done((bf16[512,768]{1,0:T(8,128)(2,1)S(1)}, bf16[512,768]{1,0:T(8,128)(2,1)S(1)}, u32[]{:S(2)}, u32[]{:S(2)}) %collective-permute-start.11) | collective-permute-done | bytes 786464 | tf_op jit(solution)/shard_map/ppermute | solution.py:333
  104.4 0.7 collective-permute-done.10
  105.1 0.5 fusion.5
  105.6 1.3 collective-permute-start.12
  106.8 0.9 collective-permute-start.13
  107.8 6.9 %down.5 = f32[2,512,768]{2,1,0:T(8,128)S(1)} custom-call(s32[8]{0:T(128)S(1)} %dynamic-slice_bitcast_fusion.ids_ref, bf16[512,2048]{1,0:T(8,128)(2,1)S(1)} %get-tuple-element.42.hidden_ref, bf16[2048,6144]{1,0:T(8,128)(2,1)} %weight_ref.7), custom_call_target="tpu_custom_call" | custom-call | flops 6442450944 | bytes 6291456 | tf_op jit(solution)/shard_map/down/pallas_call | solution.py:297
  114.6 0.0 copy-start.1
  114.6 0.0 copy-start.2
  114.6 8.2 %collective-permute-done.12 = bf16[512,768]{1,0:T(8,128)(2,1)S(1)} collective-permute-done((bf16[512,768]{1,0:T(8,128)(2,1)S(1)}, bf16[512,768]{1,0:T(8,128)(2,1)S(1)}, u32[]{:S(2)}, u32[]{:S(2)}) %collective-permute-start.12) | collective-permute-done | bytes 786464 | tf_op jit(solution)/shard_map/ppermute | solution.py:330
  122.9 0.5 fusion.3
  123.3 1.2 collective-permute-start.14
  124.6 0.9 collective-permute-start.15
  125.5 0.3 select_reduce_fusion
  125.8 4.6 %down.4 = f32[1,512,768]{2,1,0:T(8,128)S(1)} custom-call(s32[8]{0:T(128)S(1)} %dynamic-slice_bitcast_fusion.ids_ref, bf16[512,2048]{1,0:T(8,128)(2,1)S(1)} %get-tuple-element.42.hidden_ref, bf16[2048,6144]{1,0:T(8,128)(2,1)} %weight_ref.7), custom_call_target="tpu_custom_call" | custom-call | flops 3221225472 | bytes 3145728 | tf_op jit(solution)/shard_map/down/pallas_call | solution.py:297
  130.4 6.9 %collective-permute-done.14 = bf16[512,768]{1,0:T(8,128)(2,1)S(1)} collective-permute-done((bf16[512,768]{1,0:T(8,128)(2,1)S(1)}, bf16[512,768]{1,0:T(8,128)(2,1)S(1)}, u32[]{:S(2)}, u32[]{:S(2)}) %collective-permute-start.14) | collective-permute-done | bytes 786464 | tf_op jit(solution)/shard_map/ppermute | solution.py:330
  137.3 0.1 collective-permute-done.15
  137.4 2.4 %fusion.1 = bf16[1024,768]{1,0:T(8,128)(2,1)} fusion(s32[1024]{0:T(1024)S(1)} %bitcast.55, f32[1,512,768]{2,1,0:T(8,128)S(1)} %down.4, bf16[512,768]{1,0:T(8,128)(2,1)S(1)} %collective-permute-done.15, bf16[512,768]{1,0:T(8,128)(2,1)S(1)} %collective-permute-done.14, f32[512]{0:T(512)S(1)} %select_reduce_fusion), kind=kOutput, calls=%fused_computation.4 | convolution fusion | flops 808976384 | bytes 4724736 | tf_op jit(solution)/shard_map/dot_general | solution.py:25
  (13 shorter events, 0.1 us)
Async XLA Ops:
  0.0 0.7 copy-start
  3.4 20.5 %collective-permute-start = (bf16[512,768]{1,0:T(8,128)(2,1)S(1)}, bf16[512,768]{1,0:T(8,128)(2,1)S(1)}, u32[]{:S(2)}, u32[]{:S(2)}) collective-permute-start(bf16[512,768]{1,0:T(8,128)(2,1)S(1)} %get-tuple-element.30.refs_0_), channel_id=1, source_target_pairs={{0,2},{2,4},{4,6},{6,7},{7,5},{5,3},{3,1},{1,0},{8,10},{10,12},{12... | collective-permute-start | bytes 2359304 | tf_op jit(solution)/shard_map/ppermute | solution.py:330
  6.5 19.3 %collective-permute-start.4 = (bf16[512,768]{1,0:T(8,128)(2,1)S(1)}, bf16[512,768]{1,0:T(8,128)(2,1)S(1)}, u32[]{:S(2)}, u32[]{:S(2)}) collective-permute-start(bf16[512,768]{1,0:T(8,128)(2,1)S(1)} %get-tuple-element.30.refs_0_), channel_id=1, source_target_pairs={{2,0},{4,2},{6,4},{7,6},{5,7},{3,5},{1,3},{0,1},{10,8},{12,10},{14... | collective-permute-start | bytes 2359304 | tf_op jit(solution)/shard_map/ppermute | solution.py:333
  24.0 18.7 %collective-permute-start.1 = (bf16[512,768]{1,0:T(8,128)(2,1)S(1)}, bf16[512,768]{1,0:T(8,128)(2,1)S(1)}, u32[]{:S(2)}, u32[]{:S(2)}) collective-permute-start(bf16[512,768]{1,0:T(8,128)(2,1)S(1)} %collective-permute-done.refs_0_), channel_id=1, source_target_pairs={{0,2},{2,4},{4,6},{6,7},{7,5},{5,3},{3,1},{1,0},{8,10},{10,12},{12... | collective-permute-start | bytes 2359304 | tf_op jit(solution)/shard_map/ppermute | solution.py:330
  25.8 18.4 %collective-permute-start.5 = (bf16[512,768]{1,0:T(8,128)(2,1)S(1)}, bf16[512,768]{1,0:T(8,128)(2,1)S(1)}, u32[]{:S(2)}, u32[]{:S(2)}) collective-permute-start(bf16[512,768]{1,0:T(8,128)(2,1)S(1)} %collective-permute-done.4.refs_1_), channel_id=1, source_target_pairs={{2,0},{4,2},{6,4},{7,6},{5,7},{3,5},{1,3},{0,1},{10,8},{12,10},{14... | collective-permute-start | bytes 2359304 | tf_op jit(solution)/shard_map/ppermute | solution.py:333
  42.7 17.8 %collective-permute-start.2 = (bf16[512,768]{1,0:T(8,128)(2,1)S(1)}, bf16[512,768]{1,0:T(8,128)(2,1)S(1)}, u32[]{:S(2)}, u32[]{:S(2)}) collective-permute-start(bf16[512,768]{1,0:T(8,128)(2,1)S(1)} %collective-permute-done.1.refs_0_), channel_id=1, source_target_pairs={{0,2},{2,4},{4,6},{6,7},{7,5},{5,3},{3,1},{1,0},{8,10},{10,12},{12... | collective-permute-start | bytes 2359304 | tf_op jit(solution)/shard_map/ppermute | solution.py:330
  44.2 17.7 %collective-permute-start.6 = (bf16[512,768]{1,0:T(8,128)(2,1)S(1)}, bf16[512,768]{1,0:T(8,128)(2,1)S(1)}, u32[]{:S(2)}, u32[]{:S(2)}) collective-permute-start(bf16[512,768]{1,0:T(8,128)(2,1)S(1)} %collective-permute-done.5.refs_1_), channel_id=1, source_target_pairs={{2,0},{4,2},{6,4},{7,6},{5,7},{3,5},{1,3},{0,1},{10,8},{12,10},{14... | collective-permute-start | bytes 2359304 | tf_op jit(solution)/shard_map/ppermute | solution.py:333
  60.5 11.6 %collective-permute-start.3 = (bf16[256,768]{1,0:T(8,128)(2,1)S(1)}, bf16[256,768]{1,0:T(8,128)(2,1)S(1)}, u32[]{:S(2)}, u32[]{:S(2)}) collective-permute-start(bf16[256,768]{1,0:T(8,128)(2,1)S(1)} %slice.46), channel_id=1, source_target_pairs={{0,2},{2,4},{4,6},{6,7},{7,5},{5,3},{3,1},{1,0},{8,10},{10,12},{12... | collective-permute-start | bytes 1179656 | tf_op jit(solution)/shard_map/ppermute | solution.py:330
  61.9 10.2 %collective-permute-start.7 = (bf16[256,768]{1,0:T(8,128)(2,1)S(1)}, bf16[256,768]{1,0:T(8,128)(2,1)S(1)}, u32[]{:S(2)}, u32[]{:S(2)}) collective-permute-start(bf16[256,768]{1,0:T(8,128)(2,1)S(1)} %slice.47), channel_id=1, source_target_pairs={{2,0},{4,2},{6,4},{7,6},{5,7},{3,5},{1,3},{0,1},{10,8},{12,10},{14... | collective-permute-start | bytes 1179656 | tf_op jit(solution)/shard_map/ppermute | solution.py:333
  77.7 9.2 %collective-permute-start.8 = (bf16[256,768]{1,0:T(8,128)(2,1)S(1)}, bf16[256,768]{1,0:T(8,128)(2,1)S(1)}, u32[]{:S(2)}, u32[]{:S(2)}) collective-permute-start(bf16[256,768]{1,0:T(8,128)(2,1)S(1)} %get-tuple-element.43), channel_id=1, source_target_pairs={{0,2},{2,4},{4,6},{6,7},{7,5},{5,3},{3,1},{1,0},{8,10},{10,12},{12... | collective-permute-start | bytes 1179656 | tf_op jit(solution)/shard_map/ppermute | solution.py:330
  79.0 8.5 %collective-permute-start.9 = (bf16[256,768]{1,0:T(8,128)(2,1)S(1)}, bf16[256,768]{1,0:T(8,128)(2,1)S(1)}, u32[]{:S(2)}, u32[]{:S(2)}) collective-permute-start(bf16[256,768]{1,0:T(8,128)(2,1)S(1)} %get-tuple-element.44), channel_id=1, source_target_pairs={{2,0},{4,2},{6,4},{7,6},{5,7},{3,5},{1,3},{0,1},{10,8},{12,10},{14... | collective-permute-start | bytes 1179656 | tf_op jit(solution)/shard_map/ppermute | solution.py:333
  87.7 16.6 %collective-permute-start.11 = (bf16[512,768]{1,0:T(8,128)(2,1)S(1)}, bf16[512,768]{1,0:T(8,128)(2,1)S(1)}, u32[]{:S(2)}, u32[]{:S(2)}) collective-permute-start(bf16[512,768]{1,0:T(8,128)(2,1)S(1)} %pad_maximum_fusion.1), channel_id=1, source_target_pairs={{2,0},{4,2},{6,4},{7,6},{5,7},{3,5},{1,3},{0,1},{10,8},{12,10},{14... | collective-permute-start | bytes 2359304 | tf_op jit(solution)/shard_map/ppermute | solution.py:333
  88.4 16.7 %collective-permute-start.10 = (bf16[512,768]{1,0:T(8,128)(2,1)S(1)}, bf16[512,768]{1,0:T(8,128)(2,1)S(1)}, u32[]{:S(2)}, u32[]{:S(2)}) collective-permute-start(bf16[512,768]{1,0:T(8,128)(2,1)S(1)} %pad_maximum_fusion), channel_id=1, source_target_pairs={{0,2},{2,4},{4,6},{6,7},{7,5},{5,3},{3,1},{1,0},{8,10},{10,12},{12... | collective-permute-start | bytes 2359304 | tf_op jit(solution)/shard_map/ppermute | solution.py:330
  105.6 17.3 %collective-permute-start.12 = (bf16[512,768]{1,0:T(8,128)(2,1)S(1)}, bf16[512,768]{1,0:T(8,128)(2,1)S(1)}, u32[]{:S(2)}, u32[]{:S(2)}) collective-permute-start(bf16[512,768]{1,0:T(8,128)(2,1)S(1)} %get-tuple-element.56), channel_id=1, source_target_pairs={{0,2},{2,4},{4,6},{6,7},{7,5},{5,3},{3,1},{1,0},{8,10},{10,12},{12... | collective-permute-start | bytes 2359304 | tf_op jit(solution)/shard_map/ppermute | solution.py:330
  106.8 16.0 %collective-permute-start.13 = (bf16[512,768]{1,0:T(8,128)(2,1)S(1)}, bf16[512,768]{1,0:T(8,128)(2,1)S(1)}, u32[]{:S(2)}, u32[]{:S(2)}) collective-permute-start(bf16[512,768]{1,0:T(8,128)(2,1)S(1)} %get-tuple-element.55), channel_id=1, source_target_pairs={{2,0},{4,2},{6,4},{7,6},{5,7},{3,5},{1,3},{0,1},{10,8},{12,10},{14... | collective-permute-start | bytes 2359304 | tf_op jit(solution)/shard_map/ppermute | solution.py:333
  114.6 10.9 %copy-start.1 = (s32[1024,2]{0,1:T(2,128)S(1)}, s32[1024,2]{0,1:T(2,128)}, u32[]{:S(2)}) copy-start(s32[1024,2]{0,1:T(2,128)} %param.8) | copy-start | bytes 24580
  114.6 10.8 %copy-start.2 = (f32[1024,2]{0,1:T(2,128)S(1)}, f32[1024,2]{0,1:T(2,128)}, u32[]{:S(2)}) copy-start(f32[1024,2]{0,1:T(2,128)} %param.9) | copy-start | bytes 24580
  123.3 14.0 %collective-permute-start.14 = (bf16[512,768]{1,0:T(8,128)(2,1)S(1)}, bf16[512,768]{1,0:T(8,128)(2,1)S(1)}, u32[]{:S(2)}, u32[]{:S(2)}) collective-permute-start(bf16[512,768]{1,0:T(8,128)(2,1)S(1)} %get-tuple-element.54), channel_id=1, source_target_pairs={{0,2},{2,4},{4,6},{6,7},{7,5},{5,3},{3,1},{1,0},{8,10},{10,12},{12... | collective-permute-start | bytes 2359304 | tf_op jit(solution)/shard_map/ppermute | solution.py:330
  124.6 12.8 %collective-permute-start.15 = (bf16[512,768]{1,0:T(8,128)(2,1)S(1)}, bf16[512,768]{1,0:T(8,128)(2,1)S(1)}, u32[]{:S(2)}, u32[]{:S(2)}) collective-permute-start(bf16[512,768]{1,0:T(8,128)(2,1)S(1)} %get-tuple-element.53), channel_id=1, source_target_pairs={{2,0},{4,2},{6,4},{7,6},{5,7},{3,5},{1,3},{0,1},{10,8},{12,10},{14... | collective-permute-start | bytes 2359304 | tf_op jit(solution)/shard_map/ppermute | solution.py:333
